TPU v7x, 32 devices: a whole 2x2x4 slice. The times are simulated.
32 devices in a mesh: beam: 2 (over core), path: 4 (over y, x), gz: 4 (over z).
Axes of the slice: x: 2, y: 2, z: 4, core: 2. Of those that a mesh axis runs over, the one named last changes fastest.
Arguments:
- maps: float32 [8, 64, 16, 512], P(None, 'gz', 'beam', 'path'), may hold values from 0.02 to 1
- measured: float32 [8, 64, 16], P(None, 'gz', 'beam'), may hold values from 0 to 76.8
- beta_table: float32 [8, 8], replicated, may hold values from 0.3 to 2
- view: int32 [1], replicated, may hold values from 0 to 7
- kappa: float32 [16, 8], replicated, may hold values from 0.3 to 2
- line_of: int32 [8], replicated, may hold values from 0 to 15
- side: int32 [8], replicated, may hold values from 0 to 1, as said below
Outputs:
- emission: float32 [8, 64, 16], P(None, 'gz', 'beam')
- maps_out: float32 [8, 64, 16, 512], P(None, 'gz', 'beam', 'path')
- data_dual: float32 [8, 64, 16], P(None, 'gz', 'beam')
Inputs may be any that keep to these rules, and one draw needn't show every extreme that they name: Exactly 4 elements have side 0.
All inputs are finite; a program needn't handle non-finite values.
Results may differ from a plain program's by a relative error of at most 0.0001.
Values sent between devices are 32-bit elements; how exact they have to be, the bound alone decides.
No kernel may reach another device: no remote copies, remote signals or barrier semaphores. Data moves between devices by JAX's collectives and lax.ppermute only.
A program may use at most 64 MiB of HBM per device.

v0:
```python
import functools

import jax
import jax.numpy as jnp
from jax import lax
from jax.experimental import pallas as pl
from jax.experimental.pallas import tpu as pltpu
from jax.sharding import PartitionSpec as P

ITERS = 2
LAM = 0.1
F32 = jnp.float32
VMEM = pltpu.VMEM
SMEM = pltpu.SMEM
UNROLL = 4
VMEM_LIMIT = 32 * 1024 * 1024


def clip(value):
    return jnp.clip(value, -LAM, LAM)


def call(body, ins, outs, spaces, scratch=(), flops=1_000_000):
    specs = [pl.BlockSpec(memory_space=space) for space in spaces]
    moved = sum(a.size * 4 for a in ins) + sum(o.size * 4 for o in outs)
    return pl.pallas_call(
        body,
        out_shape=outs,
        in_specs=specs,
        out_specs=[pl.BlockSpec(memory_space=VMEM)] * len(outs),
        scratch_shapes=list(scratch),
        compiler_params=pltpu.CompilerParams(vmem_limit_bytes=VMEM_LIMIT),
        cost_estimate=pl.CostEstimate(flops=flops, bytes_accessed=moved, transcendentals=0),
    )(*ins)


def f32(*shape):
    return jax.ShapeDtypeStruct(shape, F32)


def shifted(block, axis, distance):
    n = lax.axis_size(axis)
    return lax.ppermute(block, axis, [((i - distance) % n, i) for i in range(n)])


def swapped(block, start):
    n, paths = lax.axis_size("gz"), lax.axis_size("path")
    route = []
    for p in range(paths):
        for z in range(n):
            other = z + 1 if (z - start) % 2 == 0 else z - 1
            there = (p, other) if 0 <= other < n else (p ^ 1, z)
            route.append((p * n + z, there[0] * n + there[1]))
    return lax.ppermute(block, ("path", "gz"), route)


def pair_order(ahead, behind):
    even = lax.rem(lax.axis_index("gz"), 2) == 0
    return jnp.where(even, ahead, behind), jnp.where(even, behind, ahead)


def merged(mine, other, far, scale, bit):
    upper = (lax.axis_index("path") & bit) != 0
    low = [jnp.where(upper, o, m) for m, o in zip(mine, other)]
    high = [jnp.where(upper, m, o) for m, o in zip(mine, other)]
    if far is None:
        return [low[0], high[1]] + [a + b for a, b in zip(low[2:], high[2:])]
    low_factor = jnp.where(far, jnp.exp(high[2] * scale), 1.0)
    high_factor = jnp.where(far, 1.0, jnp.exp(low[2] * scale))
    sums = [low_factor * a + high_factor * b for a, b in zip(low[3:], high[3:])]
    return [low[0], high[1], low[2] + high[2]] + sums


def passed(state, other, far, bit):
    mine = lax.axis_index("path")
    ahead = jnp.where(mine & (2 * bit - 1) == bit - 1, other[0], state[0])
    behind = jnp.where(mine & (2 * bit - 1) == bit, other[1], state[1])
    if far is None:
        return [ahead, behind]
    upper = (mine & bit) != 0
    in_way = jnp.where(upper, jnp.where(far, 0.0, other[2]), jnp.where(far, other[2], 0.0))
    return [ahead, behind, state[2] + in_way]


def rows_of(ref):
    return [ref[i] for i in range(ref.shape[0])]


def merge_all(bit, scale, refs, far, kept):
    mine_ref, other_ref, *state_refs = refs
    state = rows_of(state_refs[0]) if state_refs else [jnp.zeros(mine_ref.shape[1:], F32)] * kept
    mine, other = rows_of(mine_ref), rows_of(other_ref)
    return merged(mine, other, far, scale, bit), passed(state, other, far, bit)


def merge_kernel(bit, scale, kept, *refs):
    *refs, out_ref, state_ref = refs
    far = None
    if kept == 3:
        far_ref, *refs = refs
        far = far_ref[3] != 0.0
    packs, state = merge_all(bit, scale, refs, far, kept)
    for ref, values in ((out_ref, packs), (state_ref, state)):
        for i, value in enumerate(values):
            ref[i] = value


def around(block, axis, scale, far=None):
    n = lax.axis_size(axis)
    if n < 2 or n & (n - 1):
        raise ValueError("path size")
    kept = 2 if far is None else 3
    state = []
    bit = 1
    while True:
        other = lax.ppermute(block, axis, [(i, i ^ bit) for i in range(n)])
        if 2 * bit == n:
            return [block, other] + state
        ins = ([] if far is None else [far]) + [block, other] + state
        block, *state = call(
            functools.partial(merge_kernel, bit, scale, kept),
            ins,
            [f32(*block.shape), f32(kept, *block.shape[1:])],
            [VMEM] * len(ins),
        )
        bit *= 2


def split(flat):
    high = flat.astype(jnp.bfloat16)
    return high, (flat - high.astype(F32)).astype(jnp.bfloat16)


def put_rows(parts_ref, e, tiles):
    slices, cells, width = tiles.shape
    at = slice(e * slices * cells, (e + 1) * slices * cells)
    parts_ref[at, 0:width], parts_ref[at, width:] = split(tiles.reshape(slices * cells, width))


def row_sums(parts_ref, sums_ref):
    depth, width = parts_ref.shape[1], sums_ref.shape[1]
    ones = jnp.ones((depth, width), jnp.bfloat16)
    sums_ref[...] = jnp.dot(parts_ref[...], ones, preferred_element_type=F32)


def packed_sums(sums_ref, lane):
    cells, width = lane.shape
    pack = jnp.zeros((cells, width), F32)
    for k in range(sums_ref.shape[0] // cells):
        pack = jnp.where(lane == k, sums_ref[k * cells : (k + 1) * cells], pack)
    return pack


def spread(pack, lane, elems, slices, parts_ref, sums_ref):
    for e in range(elems):
        put_rows(parts_ref, e, jnp.stack([jnp.where(lane == e * slices + z, pack, 0.0) for z in range(slices)]))
    row_sums(parts_ref, sums_ref)


def tile_of(ref, k, cells):
    return ref[pl.ds(pl.multiple_of(k * cells, cells), cells)]


def gather_edges(pack, tile, lane, k):
    width = tile.shape[1]
    here = (lane == k) | (lane == (k - 1) % width)
    return jnp.where(here, pltpu.roll(tile, k, axis=1) if k else tile, pack)


def packed_edges(edges, lane):
    even = lane % 2 == 0
    first = jnp.where(even, edges[0], edges[1])
    return first, pltpu.roll(jnp.where(even, edges[1], edges[0]), 1, axis=1)


def join_edges(first, last, lane):
    width = first.shape[1]
    last = pltpu.roll(last, width - 1, axis=1)
    even = lane % 2 == 0
    return jnp.where(even, first, last), jnp.where(even, last, first)


def edge_columns(pack, rim, k):
    return jnp.where(rim, pltpu.roll(pack, pack.shape[1] - k, axis=1) if k else pack, 0.0)


def reciprocal(value):
    guess = pl.reciprocal(value, approx=True)
    return guess * (2.0 - value * guess)


def sweep(slices, body, carry):
    group = UNROLL if slices % UNROLL == 0 else slices

    def step(i, carry):
        for offset in range(group):
            carry = body(group * i + offset, offset, carry)
        return carry

    return lax.fori_loop(0, slices // group, step, carry)


def beam_sides(cells):
    count, rank = lax.axis_size("beam"), lax.axis_index("beam")
    if count == 2:
        return [
            (
                jnp.where(rank == 0, cells - 1, 0),
                jnp.where(rank == 0, F32(-1.0), F32(1.0)),
                None,
            )
        ]
    return [(cells - 1, F32(-1.0), rank < count - 1), (0, F32(1.0), rank > 0)]


def beam_rows(first, last):
    count, rank = lax.axis_size("beam"), lax.axis_index("beam")
    if count == 2:
        return [jnp.where(rank == 0, last, first)]
    return [last, first]


def face(own, other, sign, there):
    step = (own - other) * sign
    return step if there is None else jnp.where(there, step, 0.0)


def exchange_beam(rows):
    if lax.axis_size("beam") == 2:
        return [lax.ppermute(rows[0], "beam", [(0, 1), (1, 0)])]
    return [shifted(rows[1], "beam", -1), shifted(rows[0], "beam", 1)]


def open_kernel(total, view_ref, source_ref, *refs):
    small, refs = refs[:4], refs[4:]
    maps_ref, inside_ref, coef_ref, *refs = refs
    elems, slices, cells, width = maps_ref.shape
    faces = len(beam_sides(cells))
    face_refs, refs = refs[:faces], refs[faces:]
    beta_ref, kappa_ref, line_ref, side_ref, sems = refs
    half = slices // 2
    parts = [pl.ds(0, half), pl.ds(half, slices - half)] if half else [pl.ds(0, slices)]
    fetch = []
    for i, (ref, kept) in enumerate(zip(small, (beta_ref, kappa_ref, line_ref, side_ref))):
        fetch.append(pltpu.make_async_copy(ref, kept, sems.at[i]))
    large = []
    for i, at in enumerate(parts):
        large.append(pltpu.make_async_copy(source_ref.at[:, at], maps_ref.at[:, at], sems.at[len(small) + i]))
    for copy in large[:1] + fetch + large[1:]:
        copy.start()
    for copy in fetch:
        copy.wait()
    for e in range(elems):
        line = line_ref[e]
        for f in range(elems):
            coef_ref[e * elems + f : e * elems + f + 1] = jnp.full((1, width), kappa_ref[f, line])
        coef_ref[elems * elems + e : elems * elems + e + 1] = jnp.full((1, width), side_ref[e].astype(F32))
    view = view_ref[0, 0]
    beta = [beta_ref[view, e] for e in range(elems)]
    sub = lax.broadcasted_iota(jnp.int32, maps_ref.shape[2:], 0)
    for z in range(slices):
        if z == 0 or z == half:
            large[1 if z else 0].wait()
        tiles = [maps_ref[e, z] for e in range(elems)]
        mu = beta[0] * tiles[0]
        for e in range(1, elems):
            mu = mu + beta[e] * tiles[e]
        run = mu
        reach = 1
        while reach < cells:
            run = run + jnp.where(sub >= reach, pltpu.roll(run, reach, axis=0), 0.0)
            reach *= 2
        inside_ref[z] = jnp.where(sub >= 1, pltpu.roll(run, 1, axis=0), 0.0)
        face_refs[0][elems * slices + z : elems * slices + z + 1] = run[cells - 1 : cells]
        for e in range(elems):
            rows = beam_rows(tiles[e][0:1], tiles[e][cells - 1 : cells])
            for ref, row in zip(face_refs, rows):
                ref[e * slices + z : e * slices + z + 1] = row


def depth_kernel(total, maps_ref, coef_ref, local_ref, pack_ref, mu_ref, parts_ref, sums_ref):
    elems, slices, cells, width = maps_ref.shape
    rows = slices * cells
    row = lax.broadcasted_iota(jnp.int32, (2 * width, 2 * width), 0)
    col = lax.broadcasted_iota(jnp.int32, (2 * width, 2 * width), 1)
    row = jnp.where(row >= width, row - width, row)
    table = jnp.where((row < col) | (col >= width), 1.0, 0.0).astype(jnp.bfloat16)
    for e in range(elems):
        mu = coef_ref[e * elems : e * elems + 1][None] * maps_ref[0]
        for f in range(1, elems):
            mu = mu + coef_ref[e * elems + f : e * elems + f + 1][None] * maps_ref[f]
        mu_ref[e] = mu
        put_rows(parts_ref, e, mu)
    sums_ref[...] = jnp.dot(parts_ref[...], table, preferred_element_type=F32)
    lane = lax.broadcasted_iota(jnp.int32, (cells, width), 1)
    scale = -1.0 / total
    strip = jnp.zeros((cells, width), F32)
    edges = [strip, strip]
    for e in range(elems):
        forward = coef_ref[elems * elems + e : elems * elems + e + 1] == 0.0
        for z in range(slices):
            k = e * slices + z
            before = sums_ref[k * cells : (k + 1) * cells, 0:width]
            whole = sums_ref[k * cells : (k + 1) * cells, width:]
            after = whole - before - mu_ref[e, z]
            local_ref[e, z] = jnp.exp(jnp.where(forward, before, after) * scale)
            strip = jnp.where(lane == k, whole, strip)
            edges[k % 2] = gather_edges(edges[k % 2], maps_ref[e, z], lane, k)
    pack_ref[0], pack_ref[1] = packed_edges(edges, lane)
    pack_ref[2] = strip
    far = jnp.zeros((cells, width), F32)
    for e in range(elems):
        inside = (lane >= e * slices) & (lane < (e + 1) * slices)
        far = jnp.where(inside, coef_ref[elems * elems + e : elems * elems + e + 1][:, 0:1], far)
    pack_ref[3] = far


def weight_kernel(total, skip, maps_ref, inside_ref, carry_ref, local_ref, pack_ref, weight_ref, out_ref, zone_ref,
                  ztwo_ref, proj_ref, whole_ref, sums_ref):
    elems, slices, cells, width = maps_ref.shape
    lane = lax.broadcasted_iota(jnp.int32, (cells, width), 1)
    there = lax.axis_index("beam") > 0
    carry = jnp.where(there, carry_ref[skip : skip + slices], 0.0)
    att = jnp.exp((inside_ref[...] + carry[:, None]) * (-1.0 / total))
    for e in range(elems):
        weight = att * local_ref[e]
        weight_ref[e] = weight
        put_rows(whole_ref, e, weight)
        put_rows(proj_ref, e, weight * maps_ref[e])
    row_sums(proj_ref, sums_ref)
    out_ref[3] = packed_sums(sums_ref, lane)
    row_sums(whole_ref, sums_ref)
    out_ref[4] = packed_sums(sums_ref, lane)
    for i in range(3):
        out_ref[i] = pack_ref[i]
    for e in range(elems):
        zone_ref[e], ztwo_ref[e] = pair_order(maps_ref[e, slices - 1], maps_ref[e, 0])


def dual_step(field, ahead, dual, last):
    step = 0.5 * (ahead - field)
    return jnp.where(last, 0.0, clip(step if dual is None else dual + step))


def tile_duals(tile, dual_x, dual_y, sub, lane, shape):
    cells, width = shape
    new_x = dual_step(tile, pltpu.roll(tile, cells - 1, axis=0), dual_x, sub == cells - 1)
    new_y = dual_step(tile, pltpu.roll(tile, width - 1, axis=1), dual_y, lane == width - 1)
    spread = pltpu.roll(new_x, 1, axis=0) - new_x + (pltpu.roll(new_y, 1, axis=1) - new_y)
    return new_x, new_y, spread


def join(ref, width):
    elems, cells, slices = ref.shape
    parts = [ref[e] for e in range(elems)]
    if elems * slices < width:
        parts.append(jnp.zeros((cells, width - elems * slices), F32))
    return jnp.concatenate(parts, axis=1)


def first_dual_kernel(maps_ref, measured_ref, *refs):
    elems, slices, cells, width = maps_ref.shape
    sides = beam_sides(cells)
    own_refs, refs = refs[: len(sides)], refs[len(sides) :]
    other_refs, refs = refs[: len(sides)], refs[len(sides) :]
    dual_z_ref, dual_x_ref, dual_y_ref, adj_ref, still_ref, *edge_refs = refs
    sub = lax.broadcasted_iota(jnp.int32, (cells, width), 0)
    lane = lax.broadcasted_iota(jnp.int32, (cells, width), 1)
    still_ref[...] = join(measured_ref, width)
    for (row, sign, there), own, other, edge in zip(sides, own_refs, other_refs, edge_refs):
        rows = pl.ds(0, elems * slices)
        edge[...] = clip(0.5 * face(own[rows], other[rows], sign, there))
    def step(z, behind):
        at_end = z == slices - 1
        duals = []
        for e in range(elems):
            tile = maps_ref[e, z]
            ahead = maps_ref[e, jnp.minimum(z + 1, slices - 1)]
            dual_z = jnp.where(at_end, 0.0, clip(0.5 * (ahead - tile)))
            dual_x, dual_y, spread = tile_duals(tile, None, None, sub, lane, (cells, width))
            dual_z_ref[e, z] = dual_z
            dual_x_ref[e, z] = dual_x
            dual_y_ref[e, z] = dual_y
            spread = spread + (behind[e] - dual_z)
            for (row, sign, there), edge in zip(sides, edge_refs):
                spread = spread + jnp.where(sub == row, sign * edge[pl.ds(e * slices + z, 1)], 0.0)
            adj_ref[e, z] = spread
            duals.append(dual_z)
        return tuple(duals)

    zero = jnp.zeros((cells, width), F32)
    lax.fori_loop(0, slices, step, (zero,) * elems, unroll=UNROLL)


def part(ref, pack):
    slices = ref.shape[2]
    for e in range(ref.shape[0]):
        ref[e] = pack[:, e * slices : (e + 1) * slices]


def first_update_kernel(total, size, maps_ref, weight_ref, adj_ref, still_ref, far_ref, pack_ref, zone_ref, ztwo_ref,
                        *refs):
    elems, slices, cells, width = maps_ref.shape
    pack_refs, refs = refs[:-12], refs[-12:]
    full_ref, tau_ref, cur_ref, ext_ref, dd_ref, yedge_ref, zdual_ref, out_ref, emission_ref, *refs = refs
    parts_ref, own_ref, dual_ref = refs
    count, rank = lax.axis_size("gz"), lax.axis_index("gz")
    mine = lax.axis_index("path")
    pack_shape = (cells, width)
    lane = lax.broadcasted_iota(jnp.int32, pack_shape, 1)
    rim = (lane == 0) | (lane == width - 1)
    packs, state = merge_all(size // 2, -1.0 / total, pack_refs, far_ref[3] != 0.0, 3)
    image, weights = packs[3], packs[4]
    ahead, behind, base = state
    own = jnp.exp(base * (-1.0 / total))
    sig = 1.0 / weights
    data_dual = sig * (image - still_ref[...]) / (1.0 + sig)
    dd_ref[0] = data_dual
    dd_ref[1] = sig
    part(emission_ref, image * (1.0 / total))
    y_ahead = jnp.where(mine < size - 1, clip(0.5 * (ahead - pack_ref[1])), 0.0)
    y_behind = jnp.where(mine > 0, clip(0.5 * (pack_ref[0] - behind)), 0.0)
    joined = join_edges(y_behind, -y_ahead, lane)
    yedge_ref[0] = y_ahead
    yedge_ref[1] = y_behind

    def weigh(z, offset, none):
        for e in range(elems):
            k = e * slices + z
            weight = weight_ref[e, z] * tile_of(own_ref, k, cells)
            full_ref[e, z] = weight
            tau_ref[e, z] = reciprocal(weight + 6.0)
            ext_ref[e, z] = weight * tile_of(dual_ref, k, cells) + adj_ref[e, z]
        return none

    zero = jnp.zeros(pack_shape, F32)
    spread(own, lane, elems, slices, parts_ref, own_ref)
    spread(data_dual, lane, elems, slices, parts_ref, dual_ref)
    sweep(slices, weigh, 0)
    for e in range(elems):
        ahead, behind = pair_order(zone_ref[e], ztwo_ref[e])
        behind = jnp.where(rank > 0, clip(0.5 * (maps_ref[e, 0] - behind)), 0.0)
        ahead = jnp.where(rank < count - 1, clip(0.5 * (ahead - maps_ref[e, slices - 1])), 0.0)
        zdual_ref[0, e] = behind
        zdual_ref[1, e] = ahead
        ext_ref[e, 0] = ext_ref[e, 0] + behind
        ext_ref[e, slices - 1] = ext_ref[e, slices - 1] - ahead
    edges = [zero, zero]
    for z in range(slices):
        for e in range(elems):
            k = e * slices + z
            tile = maps_ref[e, z]
            step = (ext_ref[e, z] + edge_columns(joined[k % 2], rim, k)) * tau_ref[e, z]
            new = jnp.maximum(tile - step, 0.0)
            ext = 2.0 * new - tile
            cur_ref[e, z] = new
            ext_ref[e, z] = ext
            edges[k % 2] = gather_edges(edges[k % 2], ext, lane, k)
    out_ref[0], out_ref[1] = packed_edges(edges, lane)
    for e in range(elems):
        put_rows(parts_ref, e, full_ref[e] * ext_ref[e])
    row_sums(parts_ref, own_ref)
    out_ref[2] = packed_sums(own_ref, lane)
    for i in range(3, out_ref.shape[0]):
        out_ref[i] = zero


def face_kernel(ext_ref, zone_ref, ztwo_ref, *face_refs):
    elems, slices, cells, _ = ext_ref.shape
    for e in range(elems):
        for z in range(slices):
            rows = beam_rows(ext_ref[e, z, 0:1], ext_ref[e, z, cells - 1 : cells])
            for ref, row in zip(face_refs, rows):
                ref[e * slices + z : e * slices + z + 1] = row
        zone_ref[e], ztwo_ref[e] = pair_order(ext_ref[e, slices - 1], ext_ref[e, 0])


def second_dual_kernel(ext_ref, dual_z_ref, dual_x_ref, dual_y_ref, adj_ref):
    elems, slices, cells, width = ext_ref.shape
    sub = lax.broadcasted_iota(jnp.int32, (cells, width), 0)
    lane = lax.broadcasted_iota(jnp.int32, (cells, width), 1)

    def step(z, behind):
        at_end = z == slices - 1
        duals = []
        for e in range(elems):
            tile = ext_ref[e, z]
            ahead = ext_ref[e, jnp.minimum(z + 1, slices - 1)]
            dual_z = jnp.where(at_end, 0.0, clip(dual_z_ref[e, z] + 0.5 * (ahead - tile)))
            _, _, spread = tile_duals(tile, dual_x_ref[e, z], dual_y_ref[e, z], sub, lane, (cells, width))
            adj_ref[e, z] = spread + (behind[e] - dual_z)
            duals.append(dual_z)
        return tuple(duals)

    zero = jnp.zeros((cells, width), F32)
    lax.fori_loop(0, slices, step, (zero,) * elems, unroll=UNROLL)


def second_face_kernel(cur_ref, ext_ref, weight_ref, tau_ref, adj_ref, zdual_ref, zone_ref, ztwo_ref, *refs):
    elems, slices, cells, width = cur_ref.shape
    sides = beam_sides(cells)
    edge_refs, refs = refs[: len(sides)], refs[len(sides) :]
    own_refs, refs = refs[: len(sides)], refs[len(sides) :]
    other_refs, refs = refs[: len(sides)], refs[len(sides) :]
    base_ref, pull_ref, *face_refs = refs
    count, rank = lax.axis_size("gz"), lax.axis_index("gz")
    sub = lax.broadcasted_iota(jnp.int32, (cells, width), 0)
    for (row, sign, there), edge, own, other, out in zip(sides, edge_refs, own_refs, other_refs, face_refs):
        out[...] = clip(edge[...] + 0.5 * face(own[...], other[...], sign, there)) * sign
    for e in range(elems):
        ahead, behind = pair_order(zone_ref[e], ztwo_ref[e])
        behind = jnp.where(rank > 0, clip(zdual_ref[0, e] + 0.5 * (ext_ref[e, 0] - behind)), 0.0)
        ahead = clip(zdual_ref[1, e] + 0.5 * (ahead - ext_ref[e, slices - 1]))
        ahead = jnp.where(rank < count - 1, ahead, 0.0)
        for z in range(slices):
            k = e * slices + z
            adj = adj_ref[e, z]
            if z == 0:
                adj = adj + behind
            if z == slices - 1:
                adj = adj - ahead
            for (row, sign, there), out in zip(sides, face_refs):
                adj = adj + jnp.where(sub == row, out[k : k + 1], 0.0)
            tau = tau_ref[e, z]
            base_ref[e, z] = cur_ref[e, z] - tau * adj
            pull_ref[e, z] = tau * weight_ref[e, z]


def last_update_kernel(size, base_ref, pull_ref, tau_ref, still_ref, dd_ref, yedge_ref, own_pack_ref, *refs):
    elems, slices, cells, width = base_ref.shape
    *pack_refs, new_ref, dual_ref, parts_ref, sums_ref = refs
    mine = lax.axis_index("path")
    packs, (ahead, behind) = merge_all(size // 2, None, pack_refs, None, 2)
    image = packs[2]
    sig = dd_ref[1]
    data_dual = (dd_ref[0] + sig * (image - still_ref[...])) / (1.0 + sig)
    part(dual_ref, data_dual)
    y_ahead = jnp.where(mine < size - 1, clip(yedge_ref[0] + 0.5 * (ahead - own_pack_ref[1])), 0.0)
    y_behind = jnp.where(mine > 0, clip(yedge_ref[1] + 0.5 * (own_pack_ref[0] - behind)), 0.0)
    lane = lax.broadcasted_iota(jnp.int32, (cells, width), 1)
    rim = (lane == 0) | (lane == width - 1)
    joined = join_edges(y_behind, -y_ahead, lane)

    def weigh(z, offset, none):
        for e in range(elems):
            new_ref[e, z] = base_ref[e, z] - pull_ref[e, z] * tile_of(sums_ref, e * slices + z, cells)
        return none

    spread(data_dual, lane, elems, slices, parts_ref, sums_ref)
    sweep(slices, weigh, 0)
    for z in range(slices):
        for e in range(elems):
            k = e * slices + z
            edge = edge_columns(joined[k % 2], rim, k)
            new_ref[e, z] = jnp.maximum(new_ref[e, z] - edge * tau_ref[e, z], 0.0)


def shards(maps, measured, beta_table, view, kappa, line_of, side):
    elems, slices, cells, width = maps.shape
    total_x = cells * lax.axis_size("beam")
    total_y = width * lax.axis_size("path")
    size = lax.axis_size("path")
    block = f32(elems, slices, cells, width)
    plane = f32(elems, cells, width)
    rows = f32(elems * slices, width)
    faces = len(beam_sides(cells))
    measured = measured.transpose(0, 2, 1)
    kappa = kappa.T
    view = view.reshape(1, 1)

    tall = f32((elems + 1) * slices, width)
    parts = pltpu.VMEM((elems * slices * cells, 2 * width), jnp.bfloat16)
    sums = pltpu.VMEM((elems * slices * cells, width), F32)
    maps, inside, coef, *own = call(
        functools.partial(open_kernel, total_x),
        [view] + [pltpu.with_memory_space_constraint(a, pltpu.HBM) for a in (maps, beta_table, kappa, line_of, side)],
        [block, f32(slices, cells, width), f32(elems * elems + elems, width), tall] + [rows] * (faces - 1),
        [SMEM] + [pltpu.HBM] * 5,
        [
            pltpu.SMEM(beta_table.shape, F32),
            pltpu.SMEM(kappa.shape, F32),
            pltpu.SMEM(line_of.shape, jnp.int32),
            pltpu.SMEM(side.shape, jnp.int32),
            pltpu.SemaphoreType.DMA((6,)),
        ],
    )
    other = exchange_beam(own)
    carry, skip = other[-1], elems * slices
    beams = lax.axis_size("beam")
    if beams > 2:
        carry, skip = carry[skip:], 0
        reach = 1
        while reach < beams - 1:
            far = lax.axis_index("beam") > reach
            carry = carry + jnp.where(far, shifted(carry, "beam", reach), 0.0)
            reach *= 2
    local, still = call(
        functools.partial(depth_kernel, total_y),
        [maps, coef],
        [block, f32(4, cells, width)],
        [VMEM] * 2,
        [
            pltpu.VMEM(maps.shape, F32),
            parts,
            pltpu.VMEM((elems * slices * cells, 2 * width), F32),
        ],
    )
    weight, pack, zone, ztwo = call(
        functools.partial(weight_kernel, total_x, skip),
        [maps, inside, carry, local, still],
        [block, f32(5, cells, width), plane, plane],
        [VMEM] * 5,
        [parts, parts, sums],
    )
    packs = around(pack, "path", -1.0 / total_y, still)
    zone, ztwo = swapped(zone, 0), swapped(ztwo, 1)
    dual_z, dual_x, dual_y, adj, counts, *edge = call(
        first_dual_kernel,
        [maps, measured, *own, *other],
        [block, block, block, block, f32(cells, width)] + [rows] * faces,
        [VMEM] * (2 + 2 * faces),
    )
    weight, tau, current, extrap, dd, yedge, zdual, pack, emission = call(
        functools.partial(first_update_kernel, total_y, size),
        [maps, weight, adj, counts, still, pack, zone, ztwo, *packs],
        [block, block, block, block, f32(2, cells, width), f32(2, cells, width), f32(2, elems, cells, width),
         f32(5, cells, width), f32(elems, cells, slices)],
        [VMEM] * (8 + len(packs)),
        [parts, sums, sums],
    )
    packs = around(pack, "path", None)
    zone, ztwo, *own = call(face_kernel, [extrap], [plane, plane] + [rows] * faces, [VMEM])
    zone, ztwo = swapped(zone, 0), swapped(ztwo, 1)
    other = exchange_beam(own)
    (adj,) = call(second_dual_kernel, [extrap, dual_z, dual_x, dual_y], [block], [VMEM] * 4)
    base, pull = call(
        second_face_kernel,
        [current, extrap, weight, tau, adj, zdual, zone, ztwo, *edge, *own, *other],
        [block, block],
        [VMEM] * (8 + 3 * faces),
        [pltpu.VMEM((elems * slices, width), F32)] * faces,
    )
    current, data_dual = call(
        functools.partial(last_update_kernel, size),
        [base, pull, tau, counts, dd, yedge, pack, *packs],
        [block, f32(elems, cells, slices)],
        [VMEM] * (7 + len(packs)),
        [parts, sums],
    )
    return emission.transpose(0, 2, 1), current, data_dual.transpose(0, 2, 1)


def solution(mesh):
    return jax.shard_map(
        shards,
        mesh=mesh,
        in_specs=(P(None, "gz", "beam", "path"), P(None, "gz", "beam"), P(), P(), P(), P(), P()),
        out_specs=(P(None, "gz", "beam"), P(None, "gz", "beam", "path"), P(None, "gz", "beam")),
        check_vma=False,
    )
```

profile of v0, /device:TPU:0, one launch (start us, length us, event | category | flops | bytes accessed | tf_op | source)
XLA Modules:
  0.0 25.3 jit_solution(2042720965480622446)
XLA Ops:
  1.3 1.2 %shard_map.94 = (f32[8,16,8,128]{3,2,1,0:T(8,128)S(1)}, f32[16,8,128]{2,1,0:T(8,128)S(1)}, f32[72,128]{1,0:T(8,128)S(1)}, f32[144,128]{1,0:T(8,128)S(1)}) custom-call(s32[1,1]{1,0:T(1,128)} %bitcast.5.view_ref, f32[8,16,8,128]{3,2,1,0:T(8,128)} %source_ref.1, f32[8,8]{1,0:T(8,128)} %refs_0_.1, f32[8,16]{1,0:T(8,128)} %bitcast.7, s32[8]{0:T(128)} %refs_2_.1, ...), custom_call_target="tpu_custom_call" | custom-call | flops 1000000 | bytes 1225540 | tf_op jit(solution)/shard_map/pallas_call | solution.py:26
  2.5 0.5 %collective-permute-start = (f32[144,128]{1,0:T(8,128)S(1)}, f32[144,128]{1,0:T(8,128)S(1)}, u32[]{:S(2)}, u32[]{:S(2)}) collective-permute-start(f32[144,128]{1,0:T(8,128)S(1)} %get-tuple-element.41.refs_0_), channel_id=1, source_target_pairs={{0,16},{16,0},{1,17},{17,1},{2,18},{18,2},{3,19},{19,3},{4,20},{20... | collective-permute-start | bytes 221192 | tf_op jit(solution)/shard_map/ppermute | solution.py:230
  3.0 0.7 %shard_map.95 = (f32[8,16,8,128]{3,2,1,0:T(8,128)S(1)}, f32[4,8,128]{2,1,0:T(8,128)S(1)}) custom-call(f32[8,16,8,128]{3,2,1,0:T(8,128)S(1)} %get-tuple-element.39.maps_ref, f32[72,128]{1,0:T(8,128)S(1)} %get-tuple-element.42.coef_ref), custom_call_target="tpu_custom_call" | custom-call | flops 1000000 | bytes 1101824 | tf_op jit(solution)/shard_map/pallas_call | solution.py:26
  3.6 0.3 collective-permute-done.carry_ref.refs_1_
  3.9 0.5 %shard_map.96 = (f32[8,16,8,128]{3,2,1,0:T(8,128)S(1)}, f32[5,8,128]{2,1,0:T(8,128)S(1)}, f32[8,8,128]{2,1,0:T(8,128)S(1)}, f32[8,8,128]{2,1,0:T(8,128)S(1)}) custom-call(f32[8,16,8,128]{3,2,1,0:T(8,128)S(1)} %get-tuple-element.39.maps_ref, f32[16,8,128]{2,1,0:T(8,128)S(1)} %get-tuple-element.40.inside_ref, ...), custom_call_target="tpu_custom_call" | custom-call | flops 1000000 | bytes 1814528 | tf_op jit(solution)/shard_map/pallas_call | solution.py:26
  4.4 0.0 copy-start
  4.4 2.9 %collective-permute-start.3 = (f32[5,8,128]{2,1,0:T(8,128)S(1)}, f32[5,8,128]{2,1,0:T(8,128)S(1)}, u32[]{:S(2)}, u32[]{:S(2)}) collective-permute-start(f32[5,8,128]{2,1,0:T(8,128)S(1)} %get-tuple-element.48.refs_1_.pack_ref), channel_id=1, source_target_pairs={{0,4},{4,0},{8,12},{12,8},{1,5},{5,1},{9,13},{13,9},{2,6},{6,2},{1... | collective-permute-start | bytes 61448 | tf_op jit(solution)/shard_map/ppermute | solution.py:116
  7.3 1.6 %collective-permute-start.1 = (f32[8,8,128]{2,1,0:T(8,128)S(1)}, f32[8,8,128]{2,1,0:T(8,128)S(1)}, u32[]{:S(2)}, u32[]{:S(2)}) collective-permute-start(f32[8,8,128]{2,1,0:T(8,128)S(1)} %get-tuple-element.49), channel_id=1, source_target_pairs={{0,1},{1,0},{2,3},{3,2},{4,5},{5,4},{6,7},{7,6},{8,9},{9,8},{10,11... | collective-permute-start | bytes 98312 | tf_op jit(solution)/shard_map/ppermute | solution.py:54
  8.9 0.5 %collective-permute-start.2 = (f32[8,8,128]{2,1,0:T(8,128)S(1)}, f32[8,8,128]{2,1,0:T(8,128)S(1)}, u32[]{:S(2)}, u32[]{:S(2)}) collective-permute-start(f32[8,8,128]{2,1,0:T(8,128)S(1)} %get-tuple-element.50), channel_id=1, source_target_pairs={{0,4},{1,2},{2,1},{3,7},{4,0},{5,6},{6,5},{7,3},{8,12},{9,10},{10,... | collective-permute-start | bytes 98312 | tf_op jit(solution)/shard_map/ppermute | solution.py:54
  9.4 0.0 collective-permute-done.3.refs_2_
  9.4 1.8 %collective-permute-start.4 = (f32[5,8,128]{2,1,0:T(8,128)S(1)}, f32[5,8,128]{2,1,0:T(8,128)S(1)}, u32[]{:S(2)}, u32[]{:S(2)}) collective-permute-start(f32[5,8,128]{2,1,0:T(8,128)S(1)} %get-tuple-element.51.refs_0_), channel_id=1, source_target_pairs={{0,8},{4,12},{8,0},{12,4},{1,9},{5,13},{9,1},{13,5},{2,10},{6,14},... | collective-permute-start | bytes 61448 | tf_op jit(solution)/shard_map/ppermute | solution.py:116
  11.2 0.0 copy-done
  11.2 0.8 %shard_map.97 = (f32[8,16,8,128]{3,2,1,0:T(8,128)S(1)}, f32[8,16,8,128]{3,2,1,0:T(8,128)S(1)}, f32[8,16,8,128]{3,2,1,0:T(8,128)S(1)}, f32[8,16,8,128]{3,2,1,0:T(...) custom-call(f32[8,16,8,128]{3,2,1,0:T(8,128)S(1)} %get-tuple-element.39.maps_ref, f32[8,8,16]{2,1,0:T(8,128)S(1)} %bitcast.6, ...), custom_call_target="tpu_custom_call" | custom-call | flops 1000000 | bytes 2842624 | tf_op jit(solution)/shard_map/pallas_call | solution.py:26
  12.0 0.0 collective-permute-done.1.zone_ref
  12.0 0.8 %collective-permute-done.2.ztwo_ref = f32[8,8,128]{2,1,0:T(8,128)S(1)} collective-permute-done((f32[8,8,128]{2,1,0:T(8,128)S(1)}, f32[8,8,128]{2,1,0:T(8,128)S(1)}, u32[]{:S(2)}, u32[]{:S(2)}) %collective-permute-start.2) | collective-permute-done | bytes 32800 | tf_op jit(solution)/shard_map/ppermute | solution.py:54
  12.8 0.5 %collective-permute-done.4.refs_1_ = f32[5,8,128]{2,1,0:T(8,128)S(1)} collective-permute-done((f32[5,8,128]{2,1,0:T(8,128)S(1)}, f32[5,8,128]{2,1,0:T(8,128)S(1)}, u32[]{:S(2)}, u32[]{:S(2)}) %collective-permute-start.4) | collective-permute-done | bytes 20512 | tf_op jit(solution)/shard_map/ppermute | solution.py:116
  13.3 1.9 %shard_map.99 = (f32[8,16,8,128]{3,2,1,0:T(8,128)S(1)}, f32[8,16,8,128]{3,2,1,0:T(8,128)S(1)}, f32[8,16,8,128]{3,2,1,0:T(8,128)S(1)}, f32[8,16,8,128]{3,2,1,0:T(...) custom-call(f32[8,16,8,128]{3,2,1,0:T(8,128)S(1)} %get-tuple-element, ...), custom_call_target="tpu_custom_call" | custom-call | flops 1000000 | bytes 3936256 | tf_op jit(solution)/shard_map/pallas_call | solution.py:26
  15.1 0.1 shard_map.101
  15.2 0.1 collective-permute-start.7
  15.3 1.7 %collective-permute-start.8 = (f32[5,8,128]{2,1,0:T(8,128)S(1)}, f32[5,8,128]{2,1,0:T(8,128)S(1)}, u32[]{:S(2)}, u32[]{:S(2)}) collective-permute-start(f32[5,8,128]{2,1,0:T(8,128)S(1)} %get-tuple-element.70.refs_0_.own_pack_ref), channel_id=1, source_target_pairs={{0,4},{4,0},{8,12},{12,8},{1,5},{5,1},{9,13},{13,9},{2,6},{6,2},{1... | collective-permute-start | bytes 61448 | tf_op jit(solution)/shard_map/ppermute | solution.py:116
  17.0 1.6 %collective-permute-start.5 = (f32[8,8,128]{2,1,0:T(8,128)S(1)}, f32[8,8,128]{2,1,0:T(8,128)S(1)}, u32[]{:S(2)}, u32[]{:S(2)}) collective-permute-start(f32[8,8,128]{2,1,0:T(8,128)S(1)} %get-tuple-element.62), channel_id=1, source_target_pairs={{0,1},{1,0},{2,3},{3,2},{4,5},{5,4},{6,7},{7,6},{8,9},{9,8},{10,11... | collective-permute-start | bytes 98312 | tf_op jit(solution)/shard_map/ppermute | solution.py:54
  18.6 1.4 %collective-permute-start.6 = (f32[8,8,128]{2,1,0:T(8,128)S(1)}, f32[8,8,128]{2,1,0:T(8,128)S(1)}, u32[]{:S(2)}, u32[]{:S(2)}) collective-permute-start(f32[8,8,128]{2,1,0:T(8,128)S(1)} %get-tuple-element.63), channel_id=1, source_target_pairs={{0,4},{1,2},{2,1},{3,7},{4,0},{5,6},{6,5},{7,3},{8,12},{9,10},{10,... | collective-permute-start | bytes 98312 | tf_op jit(solution)/shard_map/ppermute | solution.py:54
  20.0 0.0 collective-permute-done.8.refs_1_
  20.0 1.6 %collective-permute-start.9 = (f32[5,8,128]{2,1,0:T(8,128)S(1)}, f32[5,8,128]{2,1,0:T(8,128)S(1)}, u32[]{:S(2)}, u32[]{:S(2)}) collective-permute-start(f32[5,8,128]{2,1,0:T(8,128)S(1)} %get-tuple-element.71.refs_0_), channel_id=1, source_target_pairs={{0,8},{4,12},{8,0},{12,4},{1,9},{5,13},{9,1},{13,5},{2,10},{6,14},... | collective-permute-start | bytes 61448 | tf_op jit(solution)/shard_map/ppermute | solution.py:116
  21.6 0.7 %shard_map.100.adj_ref = f32[8,16,8,128]{3,2,1,0:T(8,128)S(1)} custom-call(f32[8,16,8,128]{3,2,1,0:T(8,128)S(1)} %get-tuple-element.55.ext_ref, f32[8,16,8,128]{3,2,1,0:T(8,128)S(1)} %get-tuple-element.58.dual_z_ref, f32[8,16,8,128]{3,2,1,0:T(8,128)S(1)} %get-tuple-element.59.dual_x_ref, f32[8,16,8,128]{3,2,1,0:T(8,128)S(1)} %get-tuple-element.60.dual_y_ref), custom_call_target="tpu_custom_call" | custom-call | flops 1000000 | bytes 2621440 | tf_op jit(solution)/shard_map/pallas_call | solution.py:26
  22.3 0.0 collective-permute-done.5.zone_ref
  22.3 0.2 collective-permute-done.6.ztwo_ref
  22.5 0.0 collective-permute-done.7.refs_2_
  22.5 0.2 shard_map.102
  22.7 1.2 %collective-permute-done.9.refs_1_ = f32[5,8,128]{2,1,0:T(8,128)S(1)} collective-permute-done((f32[5,8,128]{2,1,0:T(8,128)S(1)}, f32[5,8,128]{2,1,0:T(8,128)S(1)}, u32[]{:S(2)}, u32[]{:S(2)}) %collective-permute-start.9) | collective-permute-done | bytes 20512 | tf_op jit(solution)/shard_map/ppermute | solution.py:116
  23.8 1.4 %shard_map.104 = (f32[8,16,8,128]{3,2,1,0:T(8,128)}, f32[8,8,16]{2,1,0:T(8,128)}) custom-call(f32[8,16,8,128]{3,2,1,0:T(8,128)S(1)} %get-tuple-element.66.base_ref, f32[8,16,8,128]{3,2,1,0:T(8,128)S(1)} %get-tuple-element.67.pull_ref, f32[8,16,8,128]{3,2,1,0:T(8,128)S(1)} %get-tuple-element.57.tau_ref, f32[8,128]{1,0:T(8,128)S(1)} %get-tuple-element.47.still_ref, ...), custom_call_target="tpu_custom_call" | custom-call | flops 1000000 | bytes 2191360 | tf_op jit(solution)/shard_map/pallas_call | solution.py:26
  (2 shorter events, 0.0 us)
Async XLA Ops:
  2.5 1.4 %collective-permute-start = (f32[144,128]{1,0:T(8,128)S(1)}, f32[144,128]{1,0:T(8,128)S(1)}, u32[]{:S(2)}, u32[]{:S(2)}) collective-permute-start(f32[144,128]{1,0:T(8,128)S(1)} %get-tuple-element.41.refs_0_), channel_id=1, source_target_pairs={{0,16},{16,0},{1,17},{17,1},{2,18},{18,2},{3,19},{19,3},{4,20},{20... | collective-permute-start | bytes 221192 | tf_op jit(solution)/shard_map/ppermute | solution.py:230
  4.4 6.8 %copy-start = (f32[8,16,8]{1,2,0:T(8,128)S(1)}, f32[8,16,8]{1,2,0:T(8,128)}, u32[]{:S(2)}) copy-start(f32[8,16,8]{1,2,0:T(8,128)} %param.8) | copy-start | bytes 12292
  4.4 5.0 %collective-permute-start.3 = (f32[5,8,128]{2,1,0:T(8,128)S(1)}, f32[5,8,128]{2,1,0:T(8,128)S(1)}, u32[]{:S(2)}, u32[]{:S(2)}) collective-permute-start(f32[5,8,128]{2,1,0:T(8,128)S(1)} %get-tuple-element.48.refs_1_.pack_ref), channel_id=1, source_target_pairs={{0,4},{4,0},{8,12},{12,8},{1,5},{5,1},{9,13},{13,9},{2,6},{6,2},{1... | collective-permute-start | bytes 61448 | tf_op jit(solution)/shard_map/ppermute | solution.py:116
  7.3 4.7 %collective-permute-start.1 = (f32[8,8,128]{2,1,0:T(8,128)S(1)}, f32[8,8,128]{2,1,0:T(8,128)S(1)}, u32[]{:S(2)}, u32[]{:S(2)}) collective-permute-start(f32[8,8,128]{2,1,0:T(8,128)S(1)} %get-tuple-element.49), channel_id=1, source_target_pairs={{0,1},{1,0},{2,3},{3,2},{4,5},{5,4},{6,7},{7,6},{8,9},{9,8},{10,11... | collective-permute-start | bytes 98312 | tf_op jit(solution)/shard_map/ppermute | solution.py:54
  8.9 3.9 %collective-permute-start.2 = (f32[8,8,128]{2,1,0:T(8,128)S(1)}, f32[8,8,128]{2,1,0:T(8,128)S(1)}, u32[]{:S(2)}, u32[]{:S(2)}) collective-permute-start(f32[8,8,128]{2,1,0:T(8,128)S(1)} %get-tuple-element.50), channel_id=1, source_target_pairs={{0,4},{1,2},{2,1},{3,7},{4,0},{5,6},{6,5},{7,3},{8,12},{9,10},{10,... | collective-permute-start | bytes 98312 | tf_op jit(solution)/shard_map/ppermute | solution.py:54
  9.4 3.8 %collective-permute-start.4 = (f32[5,8,128]{2,1,0:T(8,128)S(1)}, f32[5,8,128]{2,1,0:T(8,128)S(1)}, u32[]{:S(2)}, u32[]{:S(2)}) collective-permute-start(f32[5,8,128]{2,1,0:T(8,128)S(1)} %get-tuple-element.51.refs_0_), channel_id=1, source_target_pairs={{0,8},{4,12},{8,0},{12,4},{1,9},{5,13},{9,1},{13,5},{2,10},{6,14},... | collective-permute-start | bytes 61448 | tf_op jit(solution)/shard_map/ppermute | solution.py:116
  15.2 7.3 %collective-permute-start.7 = (f32[128,128]{1,0:T(8,128)S(1)}, f32[128,128]{1,0:T(8,128)S(1)}, u32[]{:S(2)}, u32[]{:S(2)}) collective-permute-start(f32[128,128]{1,0:T(8,128)S(1)} %get-tuple-element.65.refs_1_), channel_id=1, source_target_pairs={{0,16},{16,0},{1,17},{17,1},{2,18},{18,2},{3,19},{19,3},{4,20},{20... | collective-permute-start | bytes 196616 | tf_op jit(solution)/shard_map/ppermute | solution.py:230
  15.3 4.7 %collective-permute-start.8 = (f32[5,8,128]{2,1,0:T(8,128)S(1)}, f32[5,8,128]{2,1,0:T(8,128)S(1)}, u32[]{:S(2)}, u32[]{:S(2)}) collective-permute-start(f32[5,8,128]{2,1,0:T(8,128)S(1)} %get-tuple-element.70.refs_0_.own_pack_ref), channel_id=1, source_target_pairs={{0,4},{4,0},{8,12},{12,8},{1,5},{5,1},{9,13},{13,9},{2,6},{6,2},{1... | collective-permute-start | bytes 61448 | tf_op jit(solution)/shard_map/ppermute | solution.py:116
  17.0 5.3 %collective-permute-start.5 = (f32[8,8,128]{2,1,0:T(8,128)S(1)}, f32[8,8,128]{2,1,0:T(8,128)S(1)}, u32[]{:S(2)}, u32[]{:S(2)}) collective-permute-start(f32[8,8,128]{2,1,0:T(8,128)S(1)} %get-tuple-element.62), channel_id=1, source_target_pairs={{0,1},{1,0},{2,3},{3,2},{4,5},{5,4},{6,7},{7,6},{8,9},{9,8},{10,11... | collective-permute-start | bytes 98312 | tf_op jit(solution)/shard_map/ppermute | solution.py:54
  18.6 3.9 %collective-permute-start.6 = (f32[8,8,128]{2,1,0:T(8,128)S(1)}, f32[8,8,128]{2,1,0:T(8,128)S(1)}, u32[]{:S(2)}, u32[]{:S(2)}) collective-permute-start(f32[8,8,128]{2,1,0:T(8,128)S(1)} %get-tuple-element.63), channel_id=1, source_target_pairs={{0,4},{1,2},{2,1},{3,7},{4,0},{5,6},{6,5},{7,3},{8,12},{9,10},{10,... | collective-permute-start | bytes 98312 | tf_op jit(solution)/shard_map/ppermute | solution.py:54
  20.0 3.8 %collective-permute-start.9 = (f32[5,8,128]{2,1,0:T(8,128)S(1)}, f32[5,8,128]{2,1,0:T(8,128)S(1)}, u32[]{:S(2)}, u32[]{:S(2)}) collective-permute-start(f32[5,8,128]{2,1,0:T(8,128)S(1)} %get-tuple-element.71.refs_0_), channel_id=1, source_target_pairs={{0,8},{4,12},{8,0},{12,4},{1,9},{5,13},{9,1},{13,5},{2,10},{6,14},... | collective-permute-start | bytes 61448 | tf_op jit(solution)/shard_map/ppermute | solution.py:116
where the time goes:
time: 25.4 us; the launch traced here: 25.3 us
  starting transfers between devices  13.7 us (54%)
  Pallas kernels  7.35 us (29%)
  waiting for transfers between devices  2.86 us (11%)
  between operations  1.37 us (5%)
    ppermute x4, starting transfers between devices, around(): other = lax.ppermute(block, axis, [(i, i ^ bit) for i in range(n)])  7.99 us
    pallas_call x11, Pallas kernels, call(): pl.pallas_call(body, out_shape=outs, in_specs=specs, out_specs=[pl.BlockS...  7.35 us
    ppermute x4, starting transfers between devices, swapped(): return lax.ppermute(block, ('path', 'gz'), route)  5.08 us
    ppermute x4, waiting for transfers between devices, around(): other = lax.ppermute(block, axis, [(i, i ^ bit) for i in range(n)])  1.66 us
    ppermute x4, waiting for transfers between devices, swapped(): return lax.ppermute(block, ('path', 'gz'), route)  0.95 us
    ppermute x2, starting transfers between devices, exchange_beam(): return [lax.ppermute(rows[0], 'beam', [(0, 1), (1, 0)])]  0.59 us
  transfers between devices with their start and end apart: 10, of which 5 were waited for; matrix products, arithmetic and copies ran while one was open for 0% of the time, Pallas kernels for 9%

commit v1 on v0

--- a/solution.py
+++ b/solution.py
@@ -157,10 +157,6 @@
     row_sums(parts_ref, sums_ref)
 
 
-def tile_of(ref, k, cells):
-    return ref[pl.ds(pl.multiple_of(k * cells, cells), cells)]
-
-
 def gather_edges(pack, tile, lane, k):
     width = tile.shape[1]
     here = (lane == k) | (lane == (k - 1) % width)
@@ -187,17 +183,6 @@
 def reciprocal(value):
     guess = pl.reciprocal(value, approx=True)
     return guess * (2.0 - value * guess)
-
-
-def sweep(slices, body, carry):
-    group = UNROLL if slices % UNROLL == 0 else slices
-
-    def step(i, carry):
-        for offset in range(group):
-            carry = body(group * i + offset, offset, carry)
-        return carry
-
-    return lax.fori_loop(0, slices // group, step, carry)
 
 
 def beam_sides(cells):
@@ -402,7 +387,7 @@
                         *refs):
     elems, slices, cells, width = maps_ref.shape
     pack_refs, refs = refs[:-12], refs[-12:]
-    full_ref, tau_ref, cur_ref, ext_ref, dd_ref, yedge_ref, zdual_ref, out_ref, emission_ref, *refs = refs
+    pull_ref, tau_ref, cur_ref, ext_ref, dd_ref, yedge_ref, zdual_ref, out_ref, emission_ref, *refs = refs
     parts_ref, own_ref, dual_ref = refs
     count, rank = lax.axis_size("gz"), lax.axis_index("gz")
     mine = lax.axis_index("path")
@@ -424,45 +409,41 @@
     yedge_ref[0] = y_ahead
     yedge_ref[1] = y_behind
 
-    def weigh(z, offset, none):
-        for e in range(elems):
-            k = e * slices + z
-            weight = weight_ref[e, z] * tile_of(own_ref, k, cells)
-            full_ref[e, z] = weight
-            tau_ref[e, z] = reciprocal(weight + 6.0)
-            ext_ref[e, z] = weight * tile_of(dual_ref, k, cells) + adj_ref[e, z]
-        return none
-
-    zero = jnp.zeros(pack_shape, F32)
     spread(own, lane, elems, slices, parts_ref, own_ref)
     spread(data_dual, lane, elems, slices, parts_ref, dual_ref)
-    sweep(slices, weigh, 0)
+    edges = [jnp.zeros(pack_shape, F32)] * 2
     for e in range(elems):
         ahead, behind = pair_order(zone_ref[e], ztwo_ref[e])
         behind = jnp.where(rank > 0, clip(0.5 * (maps_ref[e, 0] - behind)), 0.0)
         ahead = jnp.where(rank < count - 1, clip(0.5 * (ahead - maps_ref[e, slices - 1])), 0.0)
         zdual_ref[0, e] = behind
         zdual_ref[1, e] = ahead
-        ext_ref[e, 0] = ext_ref[e, 0] + behind
-        ext_ref[e, slices - 1] = ext_ref[e, slices - 1] - ahead
-    edges = [zero, zero]
-    for z in range(slices):
-        for e in range(elems):
+        rows = []
+        for z in range(slices):
             k = e * slices + z
+            at = slice(k * cells, (k + 1) * cells)
             tile = maps_ref[e, z]
-            step = (ext_ref[e, z] + edge_columns(joined[k % 2], rim, k)) * tau_ref[e, z]
-            new = jnp.maximum(tile - step, 0.0)
+            weight = weight_ref[e, z] * own_ref[at]
+            tau = reciprocal(weight + 6.0)
+            step = weight * dual_ref[at] + adj_ref[e, z] + edge_columns(joined[k % 2], rim, k)
+            if z == 0:
+                step = step + behind
+            if z == slices - 1:
+                step = step - ahead
+            new = jnp.maximum(tile - step * tau, 0.0)
             ext = 2.0 * new - tile
+            tau_ref[e, z] = tau
+            pull_ref[e, z] = tau * weight
             cur_ref[e, z] = new
             ext_ref[e, z] = ext
+            rows.append(weight * ext)
             edges[k % 2] = gather_edges(edges[k % 2], ext, lane, k)
+        put_rows(parts_ref, e, jnp.stack(rows))
     out_ref[0], out_ref[1] = packed_edges(edges, lane)
-    for e in range(elems):
-        put_rows(parts_ref, e, full_ref[e] * ext_ref[e])
     row_sums(parts_ref, own_ref)
     out_ref[2] = packed_sums(own_ref, lane)
     for i in range(3, out_ref.shape[0]):
-        out_ref[i] = zero
+        out_ref[i] = jnp.zeros(pack_shape, F32)
 
 
 def face_kernel(ext_ref, zone_ref, ztwo_ref, *face_refs):
@@ -496,13 +477,13 @@
     lax.fori_loop(0, slices, step, (zero,) * elems, unroll=UNROLL)
 
 
-def second_face_kernel(cur_ref, ext_ref, weight_ref, tau_ref, adj_ref, zdual_ref, zone_ref, ztwo_ref, *refs):
+def second_face_kernel(cur_ref, ext_ref, tau_ref, adj_ref, zdual_ref, zone_ref, ztwo_ref, *refs):
     elems, slices, cells, width = cur_ref.shape
     sides = beam_sides(cells)
     edge_refs, refs = refs[: len(sides)], refs[len(sides) :]
     own_refs, refs = refs[: len(sides)], refs[len(sides) :]
     other_refs, refs = refs[: len(sides)], refs[len(sides) :]
-    base_ref, pull_ref, *face_refs = refs
+    base_ref, *face_refs = refs
     count, rank = lax.axis_size("gz"), lax.axis_index("gz")
     sub = lax.broadcasted_iota(jnp.int32, (cells, width), 0)
     for (row, sign, there), edge, own, other, out in zip(sides, edge_refs, own_refs, other_refs, face_refs):
@@ -521,9 +502,7 @@
                 adj = adj - ahead
             for (row, sign, there), out in zip(sides, face_refs):
                 adj = adj + jnp.where(sub == row, out[k : k + 1], 0.0)
-            tau = tau_ref[e, z]
-            base_ref[e, z] = cur_ref[e, z] - tau * adj
-            pull_ref[e, z] = tau * weight_ref[e, z]
+            base_ref[e, z] = cur_ref[e, z] - tau_ref[e, z] * adj
 
 
 def last_update_kernel(size, base_ref, pull_ref, tau_ref, still_ref, dd_ref, yedge_ref, own_pack_ref, *refs):
@@ -541,18 +520,13 @@
     rim = (lane == 0) | (lane == width - 1)
     joined = join_edges(y_behind, -y_ahead, lane)
 
-    def weigh(z, offset, none):
-        for e in range(elems):
-            new_ref[e, z] = base_ref[e, z] - pull_ref[e, z] * tile_of(sums_ref, e * slices + z, cells)
-        return none
-
     spread(data_dual, lane, elems, slices, parts_ref, sums_ref)
-    sweep(slices, weigh, 0)
-    for z in range(slices):
-        for e in range(elems):
+    for e in range(elems):
+        for z in range(slices):
             k = e * slices + z
-            edge = edge_columns(joined[k % 2], rim, k)
-            new_ref[e, z] = jnp.maximum(new_ref[e, z] - edge * tau_ref[e, z], 0.0)
+            new = base_ref[e, z] - pull_ref[e, z] * sums_ref[k * cells : (k + 1) * cells]
+            new = new - tau_ref[e, z] * edge_columns(joined[k % 2], rim, k)
+            new_ref[e, z] = jnp.maximum(new, 0.0)
 
 
 def shards(maps, measured, beta_table, view, kappa, line_of, side):
@@ -620,7 +594,7 @@
         [block, block, block, block, f32(cells, width)] + [rows] * faces,
         [VMEM] * (2 + 2 * faces),
     )
-    weight, tau, current, extrap, dd, yedge, zdual, pack, emission = call(
+    pull, tau, current, extrap, dd, yedge, zdual, pack, emission = call(
         functools.partial(first_update_kernel, total_y, size),
         [maps, weight, adj, counts, still, pack, zone, ztwo, *packs],
         [block, block, block, block, f32(2, cells, width), f32(2, cells, width), f32(2, elems, cells, width),
@@ -633,11 +607,11 @@
     zone, ztwo = swapped(zone, 0), swapped(ztwo, 1)
     other = exchange_beam(own)
     (adj,) = call(second_dual_kernel, [extrap, dual_z, dual_x, dual_y], [block], [VMEM] * 4)
-    base, pull = call(
+    (base,) = call(
         second_face_kernel,
-        [current, extrap, weight, tau, adj, zdual, zone, ztwo, *edge, *own, *other],
-        [block, block],
-        [VMEM] * (8 + 3 * faces),
+        [current, extrap, tau, adj, zdual, zone, ztwo, *edge, *own, *other],
+        [block],
+        [VMEM] * (7 + 3 * faces),
         [pltpu.VMEM((elems * slices, width), F32)] * faces,
     )
     current, data_dual = call(

time: 25.4 us -> 24.8 us (0.976)
  Pallas kernels: 7.35 us -> 6.8 us
    pallas_call x11, Pallas kernels: 7.35 us -> 6.8 us  [call(): pl.pallas_call(body, out_shape=outs, in_specs=specs, out_specs=[pl.BlockS...]
  transfers between devices with their start and end apart: 10 -> 10, of which waited for: 5 -> 5; matrix products, arithmetic and copies ran while one was open for 0% -> 0% of each run, Pallas kernels for 9% -> 10%
where the time goes in v1:
time: 24.8 us; the launch traced here: 24.7 us
  starting transfers between devices  13.7 us (55%)
  Pallas kernels  6.8 us (27%)
  waiting for transfers between devices  2.84 us (11%)
  between operations  1.37 us (6%)
    ppermute x4, starting transfers between devices, around(): other = lax.ppermute(block, axis, [(i, i ^ bit) for i in range(n)])  8 us
    pallas_call x11, Pallas kernels, call(): pl.pallas_call(body, out_shape=outs, in_specs=specs, out_specs=[pl.BlockS...  6.8 us
    ppermute x4, starting transfers between devices, swapped(): return lax.ppermute(block, ('path', 'gz'), route)  5.08 us
    ppermute x4, waiting for transfers between devices, around(): other = lax.ppermute(block, axis, [(i, i ^ bit) for i in range(n)])  1.65 us
    ppermute x4, waiting for transfers between devices, swapped(): return lax.ppermute(block, ('path', 'gz'), route)  0.94 us
    ppermute x2, starting transfers between devices, exchange_beam(): return [lax.ppermute(rows[0], 'beam', [(0, 1), (1, 0)])]  0.59 us
  transfers between devices with their start and end apart: 10, of which 5 were waited for; matrix products, arithmetic and copies ran while one was open for 0% of the time, Pallas kernels for 10%

profile of v1, /device:TPU:0, one launch (start us, length us, event | category | flops | bytes accessed | tf_op | source)
XLA Modules:
  0.0 24.7 jit_solution(572454729099249438)
XLA Ops:
  1.3 1.2 %shard_map.94 = (f32[8,16,8,128]{3,2,1,0:T(8,128)S(1)}, f32[16,8,128]{2,1,0:T(8,128)S(1)}, f32[72,128]{1,0:T(8,128)S(1)}, f32[144,128]{1,0:T(8,128)S(1)}) custom-call(s32[1,1]{1,0:T(1,128)} %bitcast.5.view_ref, f32[8,16,8,128]{3,2,1,0:T(8,128)} %source_ref.1, f32[8,8]{1,0:T(8,128)} %refs_0_.1, f32[8,16]{1,0:T(8,128)} %bitcast.7, s32[8]{0:T(128)} %refs_2_.1, ...), custom_call_target="tpu_custom_call" | custom-call | flops 1000000 | bytes 1225540 | tf_op jit(solution)/shard_map/pallas_call | solution.py:26
  2.5 0.5 %collective-permute-start = (f32[144,128]{1,0:T(8,128)S(1)}, f32[144,128]{1,0:T(8,128)S(1)}, u32[]{:S(2)}, u32[]{:S(2)}) collective-permute-start(f32[144,128]{1,0:T(8,128)S(1)} %get-tuple-element.39.refs_0_), channel_id=1, source_target_pairs={{0,16},{16,0},{1,17},{17,1},{2,18},{18,2},{3,19},{19,3},{4,20},{20... | collective-permute-start | bytes 221192 | tf_op jit(solution)/shard_map/ppermute | solution.py:215
  3.0 0.7 %shard_map.95 = (f32[8,16,8,128]{3,2,1,0:T(8,128)S(1)}, f32[4,8,128]{2,1,0:T(8,128)S(1)}) custom-call(f32[8,16,8,128]{3,2,1,0:T(8,128)S(1)} %get-tuple-element.37.maps_ref, f32[72,128]{1,0:T(8,128)S(1)} %get-tuple-element.40.coef_ref), custom_call_target="tpu_custom_call" | custom-call | flops 1000000 | bytes 1101824 | tf_op jit(solution)/shard_map/pallas_call | solution.py:26
  3.6 0.3 %collective-permute-done.carry_ref.refs_1_ = f32[144,128]{1,0:T(8,128)S(1)} collective-permute-done((f32[144,128]{1,0:T(8,128)S(1)}, f32[144,128]{1,0:T(8,128)S(1)}, u32[]{:S(2)}, u32[]{:S(2)}) %collective-permute-start) | collective-permute-done | bytes 73760 | tf_op jit(solution)/shard_map/ppermute | solution.py:215
  3.9 0.5 %shard_map.96 = (f32[8,16,8,128]{3,2,1,0:T(8,128)S(1)}, f32[5,8,128]{2,1,0:T(8,128)S(1)}, f32[8,8,128]{2,1,0:T(8,128)S(1)}, f32[8,8,128]{2,1,0:T(8,128)S(1)}) custom-call(f32[8,16,8,128]{3,2,1,0:T(8,128)S(1)} %get-tuple-element.37.maps_ref, f32[16,8,128]{2,1,0:T(8,128)S(1)} %get-tuple-element.38.inside_ref, ...), custom_call_target="tpu_custom_call" | custom-call | flops 1000000 | bytes 1814528 | tf_op jit(solution)/shard_map/pallas_call | solution.py:26
  4.4 0.0 copy-start
  4.4 2.9 %collective-permute-start.3 = (f32[5,8,128]{2,1,0:T(8,128)S(1)}, f32[5,8,128]{2,1,0:T(8,128)S(1)}, u32[]{:S(2)}, u32[]{:S(2)}) collective-permute-start(f32[5,8,128]{2,1,0:T(8,128)S(1)} %get-tuple-element.46.refs_1_.pack_ref), channel_id=1, source_target_pairs={{0,4},{4,0},{8,12},{12,8},{1,5},{5,1},{9,13},{13,9},{2,6},{6,2},{1... | collective-permute-start | bytes 61448 | tf_op jit(solution)/shard_map/ppermute | solution.py:116
  7.3 1.6 %collective-permute-start.1 = (f32[8,8,128]{2,1,0:T(8,128)S(1)}, f32[8,8,128]{2,1,0:T(8,128)S(1)}, u32[]{:S(2)}, u32[]{:S(2)}) collective-permute-start(f32[8,8,128]{2,1,0:T(8,128)S(1)} %get-tuple-element.47), channel_id=1, source_target_pairs={{0,1},{1,0},{2,3},{3,2},{4,5},{5,4},{6,7},{7,6},{8,9},{9,8},{10,11... | collective-permute-start | bytes 98312 | tf_op jit(solution)/shard_map/ppermute | solution.py:54
  8.9 0.5 %collective-permute-start.2 = (f32[8,8,128]{2,1,0:T(8,128)S(1)}, f32[8,8,128]{2,1,0:T(8,128)S(1)}, u32[]{:S(2)}, u32[]{:S(2)}) collective-permute-start(f32[8,8,128]{2,1,0:T(8,128)S(1)} %get-tuple-element.48), channel_id=1, source_target_pairs={{0,4},{1,2},{2,1},{3,7},{4,0},{5,6},{6,5},{7,3},{8,12},{9,10},{10,... | collective-permute-start | bytes 98312 | tf_op jit(solution)/shard_map/ppermute | solution.py:54
  9.4 0.0 collective-permute-done.3.refs_2_
  9.4 1.8 %collective-permute-start.4 = (f32[5,8,128]{2,1,0:T(8,128)S(1)}, f32[5,8,128]{2,1,0:T(8,128)S(1)}, u32[]{:S(2)}, u32[]{:S(2)}) collective-permute-start(f32[5,8,128]{2,1,0:T(8,128)S(1)} %get-tuple-element.49.refs_0_), channel_id=1, source_target_pairs={{0,8},{4,12},{8,0},{12,4},{1,9},{5,13},{9,1},{13,5},{2,10},{6,14},... | collective-permute-start | bytes 61448 | tf_op jit(solution)/shard_map/ppermute | solution.py:116
  11.2 0.0 copy-done
  11.2 0.8 %shard_map.97 = (f32[8,16,8,128]{3,2,1,0:T(8,128)S(1)}, f32[8,16,8,128]{3,2,1,0:T(8,128)S(1)}, f32[8,16,8,128]{3,2,1,0:T(8,128)S(1)}, f32[8,16,8,128]{3,2,1,0:T(...) custom-call(f32[8,16,8,128]{3,2,1,0:T(8,128)S(1)} %get-tuple-element.37.maps_ref, f32[8,8,16]{2,1,0:T(8,128)S(1)} %bitcast.6, ...), custom_call_target="tpu_custom_call" | custom-call | flops 1000000 | bytes 2842624 | tf_op jit(solution)/shard_map/pallas_call | solution.py:26
  12.0 0.0 collective-permute-done.1.zone_ref
  12.0 0.8 %collective-permute-done.2.ztwo_ref = f32[8,8,128]{2,1,0:T(8,128)S(1)} collective-permute-done((f32[8,8,128]{2,1,0:T(8,128)S(1)}, f32[8,8,128]{2,1,0:T(8,128)S(1)}, u32[]{:S(2)}, u32[]{:S(2)}) %collective-permute-start.2) | collective-permute-done | bytes 32800 | tf_op jit(solution)/shard_map/ppermute | solution.py:54
  12.8 0.5 %collective-permute-done.4.refs_1_ = f32[5,8,128]{2,1,0:T(8,128)S(1)} collective-permute-done((f32[5,8,128]{2,1,0:T(8,128)S(1)}, f32[5,8,128]{2,1,0:T(8,128)S(1)}, u32[]{:S(2)}, u32[]{:S(2)}) %collective-permute-start.4) | collective-permute-done | bytes 20512 | tf_op jit(solution)/shard_map/ppermute | solution.py:116
  13.3 1.6 %shard_map.99 = (f32[8,16,8,128]{3,2,1,0:T(8,128)S(1)}, f32[8,16,8,128]{3,2,1,0:T(8,128)S(1)}, f32[8,16,8,128]{3,2,1,0:T(8,128)S(1)}, f32[8,16,8,128]{3,2,1,0:T(...) custom-call(f32[8,16,8,128]{3,2,1,0:T(8,128)S(1)} %get-tuple-element, ...), custom_call_target="tpu_custom_call" | custom-call | flops 1000000 | bytes 3936256 | tf_op jit(solution)/shard_map/pallas_call | solution.py:26
  14.8 0.1 shard_map.101
  14.9 0.1 collective-permute-start.7
  15.0 1.7 %collective-permute-start.8 = (f32[5,8,128]{2,1,0:T(8,128)S(1)}, f32[5,8,128]{2,1,0:T(8,128)S(1)}, u32[]{:S(2)}, u32[]{:S(2)}) collective-permute-start(f32[5,8,128]{2,1,0:T(8,128)S(1)} %get-tuple-element.66.refs_0_.own_pack_ref), channel_id=1, source_target_pairs={{0,4},{4,0},{8,12},{12,8},{1,5},{5,1},{9,13},{13,9},{2,6},{6,2},{1... | collective-permute-start | bytes 61448 | tf_op jit(solution)/shard_map/ppermute | solution.py:116
  16.7 1.6 %collective-permute-start.5 = (f32[8,8,128]{2,1,0:T(8,128)S(1)}, f32[8,8,128]{2,1,0:T(8,128)S(1)}, u32[]{:S(2)}, u32[]{:S(2)}) collective-permute-start(f32[8,8,128]{2,1,0:T(8,128)S(1)} %get-tuple-element.59), channel_id=1, source_target_pairs={{0,1},{1,0},{2,3},{3,2},{4,5},{5,4},{6,7},{7,6},{8,9},{9,8},{10,11... | collective-permute-start | bytes 98312 | tf_op jit(solution)/shard_map/ppermute | solution.py:54
  18.3 1.4 %collective-permute-start.6 = (f32[8,8,128]{2,1,0:T(8,128)S(1)}, f32[8,8,128]{2,1,0:T(8,128)S(1)}, u32[]{:S(2)}, u32[]{:S(2)}) collective-permute-start(f32[8,8,128]{2,1,0:T(8,128)S(1)} %get-tuple-element.60), channel_id=1, source_target_pairs={{0,4},{1,2},{2,1},{3,7},{4,0},{5,6},{6,5},{7,3},{8,12},{9,10},{10,... | collective-permute-start | bytes 98312 | tf_op jit(solution)/shard_map/ppermute | solution.py:54
  19.7 0.0 collective-permute-done.8.refs_1_
  19.7 1.6 %collective-permute-start.9 = (f32[5,8,128]{2,1,0:T(8,128)S(1)}, f32[5,8,128]{2,1,0:T(8,128)S(1)}, u32[]{:S(2)}, u32[]{:S(2)}) collective-permute-start(f32[5,8,128]{2,1,0:T(8,128)S(1)} %get-tuple-element.67.refs_0_), channel_id=1, source_target_pairs={{0,8},{4,12},{8,0},{12,4},{1,9},{5,13},{9,1},{13,5},{2,10},{6,14},... | collective-permute-start | bytes 61448 | tf_op jit(solution)/shard_map/ppermute | solution.py:116
  21.3 0.7 %shard_map.100.adj_ref = f32[8,16,8,128]{3,2,1,0:T(8,128)S(1)} custom-call(f32[8,16,8,128]{3,2,1,0:T(8,128)S(1)} %get-tuple-element.53.ext_ref, f32[8,16,8,128]{3,2,1,0:T(8,128)S(1)} %get-tuple-element.55.dual_z_ref, f32[8,16,8,128]{3,2,1,0:T(8,128)S(1)} %get-tuple-element.56.dual_x_ref, f32[8,16,8,128]{3,2,1,0:T(8,128)S(1)} %get-tuple-element.57.dual_y_ref), custom_call_target="tpu_custom_call" | custom-call | flops 1000000 | bytes 2621440 | tf_op jit(solution)/shard_map/pallas_call | solution.py:26
  22.0 0.0 collective-permute-done.5.zone_ref
  22.0 0.2 collective-permute-done.6.ztwo_ref
  22.2 0.0 collective-permute-done.7.refs_2_
  22.2 0.2 shard_map.102.base_ref
  22.4 1.2 %collective-permute-done.9.refs_1_ = f32[5,8,128]{2,1,0:T(8,128)S(1)} collective-permute-done((f32[5,8,128]{2,1,0:T(8,128)S(1)}, f32[5,8,128]{2,1,0:T(8,128)S(1)}, u32[]{:S(2)}, u32[]{:S(2)}) %collective-permute-start.9) | collective-permute-done | bytes 20512 | tf_op jit(solution)/shard_map/ppermute | solution.py:116
  23.5 1.1 %shard_map.104 = (f32[8,16,8,128]{3,2,1,0:T(8,128)}, f32[8,8,16]{2,1,0:T(8,128)}) custom-call(f32[8,16,8,128]{3,2,1,0:T(8,128)S(1)} %shard_map.102.base_ref, f32[8,16,8,128]{3,2,1,0:T(8,128)S(1)} %get-tuple-element.63.pull_ref, f32[8,16,8,128]{3,2,1,0:T(8,128)S(1)} %get-tuple-element.54.tau_ref, f32[8,128]{1,0:T(8,128)S(1)} %get-tuple-element.45.still_ref, ...), custom_call_target="tpu_custom_call" | custom-call | flops 1000000 | bytes 2191360 | tf_op jit(solution)/shard_map/pallas_call | solution.py:26
  (2 shorter events, 0.0 us)
Async XLA Ops:
  2.5 1.4 %collective-permute-start = (f32[144,128]{1,0:T(8,128)S(1)}, f32[144,128]{1,0:T(8,128)S(1)}, u32[]{:S(2)}, u32[]{:S(2)}) collective-permute-start(f32[144,128]{1,0:T(8,128)S(1)} %get-tuple-element.39.refs_0_), channel_id=1, source_target_pairs={{0,16},{16,0},{1,17},{17,1},{2,18},{18,2},{3,19},{19,3},{4,20},{20... | collective-permute-start | bytes 221192 | tf_op jit(solution)/shard_map/ppermute | solution.py:215
  4.4 6.8 %copy-start = (f32[8,16,8]{1,2,0:T(8,128)S(1)}, f32[8,16,8]{1,2,0:T(8,128)}, u32[]{:S(2)}) copy-start(f32[8,16,8]{1,2,0:T(8,128)} %param.8) | copy-start | bytes 12292
  4.4 5.0 %collective-permute-start.3 = (f32[5,8,128]{2,1,0:T(8,128)S(1)}, f32[5,8,128]{2,1,0:T(8,128)S(1)}, u32[]{:S(2)}, u32[]{:S(2)}) collective-permute-start(f32[5,8,128]{2,1,0:T(8,128)S(1)} %get-tuple-element.46.refs_1_.pack_ref), channel_id=1, source_target_pairs={{0,4},{4,0},{8,12},{12,8},{1,5},{5,1},{9,13},{13,9},{2,6},{6,2},{1... | collective-permute-start | bytes 61448 | tf_op jit(solution)/shard_map/ppermute | solution.py:116
  7.3 4.7 %collective-permute-start.1 = (f32[8,8,128]{2,1,0:T(8,128)S(1)}, f32[8,8,128]{2,1,0:T(8,128)S(1)}, u32[]{:S(2)}, u32[]{:S(2)}) collective-permute-start(f32[8,8,128]{2,1,0:T(8,128)S(1)} %get-tuple-element.47), channel_id=1, source_target_pairs={{0,1},{1,0},{2,3},{3,2},{4,5},{5,4},{6,7},{7,6},{8,9},{9,8},{10,11... | collective-permute-start | bytes 98312 | tf_op jit(solution)/shard_map/ppermute | solution.py:54
  8.9 3.9 %collective-permute-start.2 = (f32[8,8,128]{2,1,0:T(8,128)S(1)}, f32[8,8,128]{2,1,0:T(8,128)S(1)}, u32[]{:S(2)}, u32[]{:S(2)}) collective-permute-start(f32[8,8,128]{2,1,0:T(8,128)S(1)} %get-tuple-element.48), channel_id=1, source_target_pairs={{0,4},{1,2},{2,1},{3,7},{4,0},{5,6},{6,5},{7,3},{8,12},{9,10},{10,... | collective-permute-start | bytes 98312 | tf_op jit(solution)/shard_map/ppermute | solution.py:54
  9.4 3.8 %collective-permute-start.4 = (f32[5,8,128]{2,1,0:T(8,128)S(1)}, f32[5,8,128]{2,1,0:T(8,128)S(1)}, u32[]{:S(2)}, u32[]{:S(2)}) collective-permute-start(f32[5,8,128]{2,1,0:T(8,128)S(1)} %get-tuple-element.49.refs_0_), channel_id=1, source_target_pairs={{0,8},{4,12},{8,0},{12,4},{1,9},{5,13},{9,1},{13,5},{2,10},{6,14},... | collective-permute-start | bytes 61448 | tf_op jit(solution)/shard_map/ppermute | solution.py:116
  14.9 7.3 %collective-permute-start.7 = (f32[128,128]{1,0:T(8,128)S(1)}, f32[128,128]{1,0:T(8,128)S(1)}, u32[]{:S(2)}, u32[]{:S(2)}) collective-permute-start(f32[128,128]{1,0:T(8,128)S(1)} %get-tuple-element.62.refs_1_), channel_id=1, source_target_pairs={{0,16},{16,0},{1,17},{17,1},{2,18},{18,2},{3,19},{19,3},{4,20},{20... | collective-permute-start | bytes 196616 | tf_op jit(solution)/shard_map/ppermute | solution.py:215
  15.0 4.7 %collective-permute-start.8 = (f32[5,8,128]{2,1,0:T(8,128)S(1)}, f32[5,8,128]{2,1,0:T(8,128)S(1)}, u32[]{:S(2)}, u32[]{:S(2)}) collective-permute-start(f32[5,8,128]{2,1,0:T(8,128)S(1)} %get-tuple-element.66.refs_0_.own_pack_ref), channel_id=1, source_target_pairs={{0,4},{4,0},{8,12},{12,8},{1,5},{5,1},{9,13},{13,9},{2,6},{6,2},{1... | collective-permute-start | bytes 61448 | tf_op jit(solution)/shard_map/ppermute | solution.py:116
  16.7 5.3 %collective-permute-start.5 = (f32[8,8,128]{2,1,0:T(8,128)S(1)}, f32[8,8,128]{2,1,0:T(8,128)S(1)}, u32[]{:S(2)}, u32[]{:S(2)}) collective-permute-start(f32[8,8,128]{2,1,0:T(8,128)S(1)} %get-tuple-element.59), channel_id=1, source_target_pairs={{0,1},{1,0},{2,3},{3,2},{4,5},{5,4},{6,7},{7,6},{8,9},{9,8},{10,11... | collective-permute-start | bytes 98312 | tf_op jit(solution)/shard_map/ppermute | solution.py:54
  18.3 3.9 %collective-permute-start.6 = (f32[8,8,128]{2,1,0:T(8,128)S(1)}, f32[8,8,128]{2,1,0:T(8,128)S(1)}, u32[]{:S(2)}, u32[]{:S(2)}) collective-permute-start(f32[8,8,128]{2,1,0:T(8,128)S(1)} %get-tuple-element.60), channel_id=1, source_target_pairs={{0,4},{1,2},{2,1},{3,7},{4,0},{5,6},{6,5},{7,3},{8,12},{9,10},{10,... | collective-permute-start | bytes 98312 | tf_op jit(solution)/shard_map/ppermute | solution.py:54
  19.7 3.8 %collective-permute-start.9 = (f32[5,8,128]{2,1,0:T(8,128)S(1)}, f32[5,8,128]{2,1,0:T(8,128)S(1)}, u32[]{:S(2)}, u32[]{:S(2)}) collective-permute-start(f32[5,8,128]{2,1,0:T(8,128)S(1)} %get-tuple-element.67.refs_0_), channel_id=1, source_target_pairs={{0,8},{4,12},{8,0},{12,4},{1,9},{5,13},{9,1},{13,5},{2,10},{6,14},... | collective-permute-start | bytes 61448 | tf_op jit(solution)/shard_map/ppermute | solution.py:116

commit v2 on v1

--- a/solution.py
+++ b/solution.py
@@ -13,6 +13,7 @@
 VMEM = pltpu.VMEM
 SMEM = pltpu.SMEM
 UNROLL = 4
+PARTS = 4
 VMEM_LIMIT = 32 * 1024 * 1024
 
 
@@ -223,8 +224,8 @@
     faces = len(beam_sides(cells))
     face_refs, refs = refs[:faces], refs[faces:]
     beta_ref, kappa_ref, line_ref, side_ref, sems = refs
-    half = slices // 2
-    parts = [pl.ds(0, half), pl.ds(half, slices - half)] if half else [pl.ds(0, slices)]
+    piece = slices // PARTS if slices % PARTS == 0 else slices
+    parts = [pl.ds(z, piece) for z in range(0, slices, piece)]
     fetch = []
     for i, (ref, kept) in enumerate(zip(small, (beta_ref, kappa_ref, line_ref, side_ref))):
         fetch.append(pltpu.make_async_copy(ref, kept, sems.at[i]))
@@ -244,8 +245,8 @@
     beta = [beta_ref[view, e] for e in range(elems)]
     sub = lax.broadcasted_iota(jnp.int32, maps_ref.shape[2:], 0)
     for z in range(slices):
-        if z == 0 or z == half:
-            large[1 if z else 0].wait()
+        if z % piece == 0:
+            large[z // piece].wait()
         tiles = [maps_ref[e, z] for e in range(elems)]
         mu = beta[0] * tiles[0]
         for e in range(1, elems):
@@ -555,7 +556,7 @@
             pltpu.SMEM(kappa.shape, F32),
             pltpu.SMEM(line_of.shape, jnp.int32),
             pltpu.SMEM(side.shape, jnp.int32),
-            pltpu.SemaphoreType.DMA((6,)),
+            pltpu.SemaphoreType.DMA((4 + PARTS,)),
         ],
     )
     other = exchange_beam(own)

time: 24.8 us -> 24.9 us (level)
  no operation moved by 1% of the time
where the time goes in v2:
time: 24.9 us; the launch traced here: 24.7 us
  starting transfers between devices  13.7 us (55%)
  Pallas kernels  6.84 us (27%)
  waiting for transfers between devices  2.85 us (11%)
  between operations  1.37 us (6%)
    ppermute x4, starting transfers between devices, around(): other = lax.ppermute(block, axis, [(i, i ^ bit) for i in range(n)])  7.97 us
    pallas_call x11, Pallas kernels, call(): pl.pallas_call(body, out_shape=outs, in_specs=specs, out_specs=[pl.BlockS...  6.84 us
    ppermute x4, starting transfers between devices, swapped(): return lax.ppermute(block, ('path', 'gz'), route)  5.1 us
    ppermute x4, waiting for transfers between devices, around(): other = lax.ppermute(block, axis, [(i, i ^ bit) for i in range(n)])  1.66 us
    ppermute x4, waiting for transfers between devices, swapped(): return lax.ppermute(block, ('path', 'gz'), route)  0.94 us
    ppermute x2, starting transfers between devices, exchange_beam(): return [lax.ppermute(rows[0], 'beam', [(0, 1), (1, 0)])]  0.59 us
  transfers between devices with their start and end apart: 10, of which 5 were waited for; matrix products, arithmetic and copies ran while one was open for 0% of the time, Pallas kernels for 10%

profile of v2, /device:TPU:0, one launch (start us, length us, event | category | flops | bytes accessed | tf_op | source)
XLA Modules:
  0.0 24.7 jit_solution(16130432587725244033)
XLA Ops:
  1.3 1.2 %shard_map.94 = (f32[8,16,8,128]{3,2,1,0:T(8,128)S(1)}, f32[16,8,128]{2,1,0:T(8,128)S(1)}, f32[72,128]{1,0:T(8,128)S(1)}, f32[144,128]{1,0:T(8,128)S(1)}) custom-call(s32[1,1]{1,0:T(1,128)} %bitcast.5.view_ref, f32[8,16,8,128]{3,2,1,0:T(8,128)} %source_ref.1, f32[8,8]{1,0:T(8,128)} %refs_0_.1, f32[8,16]{1,0:T(8,128)} %bitcast.7, s32[8]{0:T(128)} %refs_2_.1, ...), custom_call_target="tpu_custom_call" | custom-call | flops 1000000 | bytes 1225540 | tf_op jit(solution)/shard_map/pallas_call | solution.py:27
  2.5 0.5 %collective-permute-start = (f32[144,128]{1,0:T(8,128)S(1)}, f32[144,128]{1,0:T(8,128)S(1)}, u32[]{:S(2)}, u32[]{:S(2)}) collective-permute-start(f32[144,128]{1,0:T(8,128)S(1)} %get-tuple-element.39.refs_0_), channel_id=1, source_target_pairs={{0,16},{16,0},{1,17},{17,1},{2,18},{18,2},{3,19},{19,3},{4,20},{20... | collective-permute-start | bytes 221192 | tf_op jit(solution)/shard_map/ppermute | solution.py:216
  3.0 0.7 %shard_map.95 = (f32[8,16,8,128]{3,2,1,0:T(8,128)S(1)}, f32[4,8,128]{2,1,0:T(8,128)S(1)}) custom-call(f32[8,16,8,128]{3,2,1,0:T(8,128)S(1)} %get-tuple-element.37.maps_ref, f32[72,128]{1,0:T(8,128)S(1)} %get-tuple-element.40.coef_ref), custom_call_target="tpu_custom_call" | custom-call | flops 1000000 | bytes 1101824 | tf_op jit(solution)/shard_map/pallas_call | solution.py:27
  3.7 0.3 %collective-permute-done.carry_ref.refs_1_ = f32[144,128]{1,0:T(8,128)S(1)} collective-permute-done((f32[144,128]{1,0:T(8,128)S(1)}, f32[144,128]{1,0:T(8,128)S(1)}, u32[]{:S(2)}, u32[]{:S(2)}) %collective-permute-start) | collective-permute-done | bytes 73760 | tf_op jit(solution)/shard_map/ppermute | solution.py:216
  3.9 0.5 %shard_map.96 = (f32[8,16,8,128]{3,2,1,0:T(8,128)S(1)}, f32[5,8,128]{2,1,0:T(8,128)S(1)}, f32[8,8,128]{2,1,0:T(8,128)S(1)}, f32[8,8,128]{2,1,0:T(8,128)S(1)}) custom-call(f32[8,16,8,128]{3,2,1,0:T(8,128)S(1)} %get-tuple-element.37.maps_ref, f32[16,8,128]{2,1,0:T(8,128)S(1)} %get-tuple-element.38.inside_ref, ...), custom_call_target="tpu_custom_call" | custom-call | flops 1000000 | bytes 1814528 | tf_op jit(solution)/shard_map/pallas_call | solution.py:27
  4.4 0.0 copy-start
  4.4 2.9 %collective-permute-start.3 = (f32[5,8,128]{2,1,0:T(8,128)S(1)}, f32[5,8,128]{2,1,0:T(8,128)S(1)}, u32[]{:S(2)}, u32[]{:S(2)}) collective-permute-start(f32[5,8,128]{2,1,0:T(8,128)S(1)} %get-tuple-element.46.refs_1_.pack_ref), channel_id=1, source_target_pairs={{0,4},{4,0},{8,12},{12,8},{1,5},{5,1},{9,13},{13,9},{2,6},{6,2},{1... | collective-permute-start | bytes 61448 | tf_op jit(solution)/shard_map/ppermute | solution.py:117
  7.3 1.6 %collective-permute-start.1 = (f32[8,8,128]{2,1,0:T(8,128)S(1)}, f32[8,8,128]{2,1,0:T(8,128)S(1)}, u32[]{:S(2)}, u32[]{:S(2)}) collective-permute-start(f32[8,8,128]{2,1,0:T(8,128)S(1)} %get-tuple-element.47), channel_id=1, source_target_pairs={{0,1},{1,0},{2,3},{3,2},{4,5},{5,4},{6,7},{7,6},{8,9},{9,8},{10,11... | collective-permute-start | bytes 98312 | tf_op jit(solution)/shard_map/ppermute | solution.py:55
  8.9 0.5 %collective-permute-start.2 = (f32[8,8,128]{2,1,0:T(8,128)S(1)}, f32[8,8,128]{2,1,0:T(8,128)S(1)}, u32[]{:S(2)}, u32[]{:S(2)}) collective-permute-start(f32[8,8,128]{2,1,0:T(8,128)S(1)} %get-tuple-element.48), channel_id=1, source_target_pairs={{0,4},{1,2},{2,1},{3,7},{4,0},{5,6},{6,5},{7,3},{8,12},{9,10},{10,... | collective-permute-start | bytes 98312 | tf_op jit(solution)/shard_map/ppermute | solution.py:55
  9.4 0.0 collective-permute-done.3.refs_2_
  9.4 1.8 %collective-permute-start.4 = (f32[5,8,128]{2,1,0:T(8,128)S(1)}, f32[5,8,128]{2,1,0:T(8,128)S(1)}, u32[]{:S(2)}, u32[]{:S(2)}) collective-permute-start(f32[5,8,128]{2,1,0:T(8,128)S(1)} %get-tuple-element.49.refs_0_), channel_id=1, source_target_pairs={{0,8},{4,12},{8,0},{12,4},{1,9},{5,13},{9,1},{13,5},{2,10},{6,14},... | collective-permute-start | bytes 61448 | tf_op jit(solution)/shard_map/ppermute | solution.py:117
  11.2 0.0 copy-done
  11.2 0.8 %shard_map.97 = (f32[8,16,8,128]{3,2,1,0:T(8,128)S(1)}, f32[8,16,8,128]{3,2,1,0:T(8,128)S(1)}, f32[8,16,8,128]{3,2,1,0:T(8,128)S(1)}, f32[8,16,8,128]{3,2,1,0:T(...) custom-call(f32[8,16,8,128]{3,2,1,0:T(8,128)S(1)} %get-tuple-element.37.maps_ref, f32[8,8,16]{2,1,0:T(8,128)S(1)} %bitcast.6, ...), custom_call_target="tpu_custom_call" | custom-call | flops 1000000 | bytes 2842624 | tf_op jit(solution)/shard_map/pallas_call | solution.py:27
  12.0 0.0 collective-permute-done.1.zone_ref
  12.0 0.8 %collective-permute-done.2.ztwo_ref = f32[8,8,128]{2,1,0:T(8,128)S(1)} collective-permute-done((f32[8,8,128]{2,1,0:T(8,128)S(1)}, f32[8,8,128]{2,1,0:T(8,128)S(1)}, u32[]{:S(2)}, u32[]{:S(2)}) %collective-permute-start.2) | collective-permute-done | bytes 32800 | tf_op jit(solution)/shard_map/ppermute | solution.py:55
  12.8 0.5 %collective-permute-done.4.refs_1_ = f32[5,8,128]{2,1,0:T(8,128)S(1)} collective-permute-done((f32[5,8,128]{2,1,0:T(8,128)S(1)}, f32[5,8,128]{2,1,0:T(8,128)S(1)}, u32[]{:S(2)}, u32[]{:S(2)}) %collective-permute-start.4) | collective-permute-done | bytes 20512 | tf_op jit(solution)/shard_map/ppermute | solution.py:117
  13.3 1.6 %shard_map.99 = (f32[8,16,8,128]{3,2,1,0:T(8,128)S(1)}, f32[8,16,8,128]{3,2,1,0:T(8,128)S(1)}, f32[8,16,8,128]{3,2,1,0:T(8,128)S(1)}, f32[8,16,8,128]{3,2,1,0:T(...) custom-call(f32[8,16,8,128]{3,2,1,0:T(8,128)S(1)} %get-tuple-element, ...), custom_call_target="tpu_custom_call" | custom-call | flops 1000000 | bytes 3936256 | tf_op jit(solution)/shard_map/pallas_call | solution.py:27
  14.8 0.1 shard_map.101
  14.9 0.1 collective-permute-start.7
  15.0 1.7 %collective-permute-start.8 = (f32[5,8,128]{2,1,0:T(8,128)S(1)}, f32[5,8,128]{2,1,0:T(8,128)S(1)}, u32[]{:S(2)}, u32[]{:S(2)}) collective-permute-start(f32[5,8,128]{2,1,0:T(8,128)S(1)} %get-tuple-element.66.refs_0_.own_pack_ref), channel_id=1, source_target_pairs={{0,4},{4,0},{8,12},{12,8},{1,5},{5,1},{9,13},{13,9},{2,6},{6,2},{1... | collective-permute-start | bytes 61448 | tf_op jit(solution)/shard_map/ppermute | solution.py:117
  16.7 1.6 %collective-permute-start.5 = (f32[8,8,128]{2,1,0:T(8,128)S(1)}, f32[8,8,128]{2,1,0:T(8,128)S(1)}, u32[]{:S(2)}, u32[]{:S(2)}) collective-permute-start(f32[8,8,128]{2,1,0:T(8,128)S(1)} %get-tuple-element.59), channel_id=1, source_target_pairs={{0,1},{1,0},{2,3},{3,2},{4,5},{5,4},{6,7},{7,6},{8,9},{9,8},{10,11... | collective-permute-start | bytes 98312 | tf_op jit(solution)/shard_map/ppermute | solution.py:55
  18.3 1.4 %collective-permute-start.6 = (f32[8,8,128]{2,1,0:T(8,128)S(1)}, f32[8,8,128]{2,1,0:T(8,128)S(1)}, u32[]{:S(2)}, u32[]{:S(2)}) collective-permute-start(f32[8,8,128]{2,1,0:T(8,128)S(1)} %get-tuple-element.60), channel_id=1, source_target_pairs={{0,4},{1,2},{2,1},{3,7},{4,0},{5,6},{6,5},{7,3},{8,12},{9,10},{10,... | collective-permute-start | bytes 98312 | tf_op jit(solution)/shard_map/ppermute | solution.py:55
  19.7 0.0 collective-permute-done.8.refs_1_
  19.7 1.6 %collective-permute-start.9 = (f32[5,8,128]{2,1,0:T(8,128)S(1)}, f32[5,8,128]{2,1,0:T(8,128)S(1)}, u32[]{:S(2)}, u32[]{:S(2)}) collective-permute-start(f32[5,8,128]{2,1,0:T(8,128)S(1)} %get-tuple-element.67.refs_0_), channel_id=1, source_target_pairs={{0,8},{4,12},{8,0},{12,4},{1,9},{5,13},{9,1},{13,5},{2,10},{6,14},... | collective-permute-start | bytes 61448 | tf_op jit(solution)/shard_map/ppermute | solution.py:117
  21.3 0.7 %shard_map.100.adj_ref = f32[8,16,8,128]{3,2,1,0:T(8,128)S(1)} custom-call(f32[8,16,8,128]{3,2,1,0:T(8,128)S(1)} %get-tuple-element.53.ext_ref, f32[8,16,8,128]{3,2,1,0:T(8,128)S(1)} %get-tuple-element.55.dual_z_ref, f32[8,16,8,128]{3,2,1,0:T(8,128)S(1)} %get-tuple-element.56.dual_x_ref, f32[8,16,8,128]{3,2,1,0:T(8,128)S(1)} %get-tuple-element.57.dual_y_ref), custom_call_target="tpu_custom_call" | custom-call | flops 1000000 | bytes 2621440 | tf_op jit(solution)/shard_map/pallas_call | solution.py:27
  22.1 0.0 collective-permute-done.5.zone_ref
  22.1 0.2 collective-permute-done.6.ztwo_ref
  22.2 0.0 collective-permute-done.7.refs_2_
  22.2 0.2 shard_map.102.base_ref
  22.4 1.2 %collective-permute-done.9.refs_1_ = f32[5,8,128]{2,1,0:T(8,128)S(1)} collective-permute-done((f32[5,8,128]{2,1,0:T(8,128)S(1)}, f32[5,8,128]{2,1,0:T(8,128)S(1)}, u32[]{:S(2)}, u32[]{:S(2)}) %collective-permute-start.9) | collective-permute-done | bytes 20512 | tf_op jit(solution)/shard_map/ppermute | solution.py:117
  23.6 1.1 %shard_map.104 = (f32[8,16,8,128]{3,2,1,0:T(8,128)}, f32[8,8,16]{2,1,0:T(8,128)}) custom-call(f32[8,16,8,128]{3,2,1,0:T(8,128)S(1)} %shard_map.102.base_ref, f32[8,16,8,128]{3,2,1,0:T(8,128)S(1)} %get-tuple-element.63.pull_ref, f32[8,16,8,128]{3,2,1,0:T(8,128)S(1)} %get-tuple-element.54.tau_ref, f32[8,128]{1,0:T(8,128)S(1)} %get-tuple-element.45.still_ref, ...), custom_call_target="tpu_custom_call" | custom-call | flops 1000000 | bytes 2191360 | tf_op jit(solution)/shard_map/pallas_call | solution.py:27
  (2 shorter events, 0.0 us)
Async XLA Ops:
  2.5 1.4 %collective-permute-start = (f32[144,128]{1,0:T(8,128)S(1)}, f32[144,128]{1,0:T(8,128)S(1)}, u32[]{:S(2)}, u32[]{:S(2)}) collective-permute-start(f32[144,128]{1,0:T(8,128)S(1)} %get-tuple-element.39.refs_0_), channel_id=1, source_target_pairs={{0,16},{16,0},{1,17},{17,1},{2,18},{18,2},{3,19},{19,3},{4,20},{20... | collective-permute-start | bytes 221192 | tf_op jit(solution)/shard_map/ppermute | solution.py:216
  4.4 6.8 %copy-start = (f32[8,16,8]{1,2,0:T(8,128)S(1)}, f32[8,16,8]{1,2,0:T(8,128)}, u32[]{:S(2)}) copy-start(f32[8,16,8]{1,2,0:T(8,128)} %param.8) | copy-start | bytes 12292
  4.4 5.0 %collective-permute-start.3 = (f32[5,8,128]{2,1,0:T(8,128)S(1)}, f32[5,8,128]{2,1,0:T(8,128)S(1)}, u32[]{:S(2)}, u32[]{:S(2)}) collective-permute-start(f32[5,8,128]{2,1,0:T(8,128)S(1)} %get-tuple-element.46.refs_1_.pack_ref), channel_id=1, source_target_pairs={{0,4},{4,0},{8,12},{12,8},{1,5},{5,1},{9,13},{13,9},{2,6},{6,2},{1... | collective-permute-start | bytes 61448 | tf_op jit(solution)/shard_map/ppermute | solution.py:117
  7.3 4.7 %collective-permute-start.1 = (f32[8,8,128]{2,1,0:T(8,128)S(1)}, f32[8,8,128]{2,1,0:T(8,128)S(1)}, u32[]{:S(2)}, u32[]{:S(2)}) collective-permute-start(f32[8,8,128]{2,1,0:T(8,128)S(1)} %get-tuple-element.47), channel_id=1, source_target_pairs={{0,1},{1,0},{2,3},{3,2},{4,5},{5,4},{6,7},{7,6},{8,9},{9,8},{10,11... | collective-permute-start | bytes 98312 | tf_op jit(solution)/shard_map/ppermute | solution.py:55
  8.9 3.9 %collective-permute-start.2 = (f32[8,8,128]{2,1,0:T(8,128)S(1)}, f32[8,8,128]{2,1,0:T(8,128)S(1)}, u32[]{:S(2)}, u32[]{:S(2)}) collective-permute-start(f32[8,8,128]{2,1,0:T(8,128)S(1)} %get-tuple-element.48), channel_id=1, source_target_pairs={{0,4},{1,2},{2,1},{3,7},{4,0},{5,6},{6,5},{7,3},{8,12},{9,10},{10,... | collective-permute-start | bytes 98312 | tf_op jit(solution)/shard_map/ppermute | solution.py:55
  9.4 3.8 %collective-permute-start.4 = (f32[5,8,128]{2,1,0:T(8,128)S(1)}, f32[5,8,128]{2,1,0:T(8,128)S(1)}, u32[]{:S(2)}, u32[]{:S(2)}) collective-permute-start(f32[5,8,128]{2,1,0:T(8,128)S(1)} %get-tuple-element.49.refs_0_), channel_id=1, source_target_pairs={{0,8},{4,12},{8,0},{12,4},{1,9},{5,13},{9,1},{13,5},{2,10},{6,14},... | collective-permute-start | bytes 61448 | tf_op jit(solution)/shard_map/ppermute | solution.py:117
  14.9 7.3 %collective-permute-start.7 = (f32[128,128]{1,0:T(8,128)S(1)}, f32[128,128]{1,0:T(8,128)S(1)}, u32[]{:S(2)}, u32[]{:S(2)}) collective-permute-start(f32[128,128]{1,0:T(8,128)S(1)} %get-tuple-element.62.refs_1_), channel_id=1, source_target_pairs={{0,16},{16,0},{1,17},{17,1},{2,18},{18,2},{3,19},{19,3},{4,20},{20... | collective-permute-start | bytes 196616 | tf_op jit(solution)/shard_map/ppermute | solution.py:216
  15.0 4.7 %collective-permute-start.8 = (f32[5,8,128]{2,1,0:T(8,128)S(1)}, f32[5,8,128]{2,1,0:T(8,128)S(1)}, u32[]{:S(2)}, u32[]{:S(2)}) collective-permute-start(f32[5,8,128]{2,1,0:T(8,128)S(1)} %get-tuple-element.66.refs_0_.own_pack_ref), channel_id=1, source_target_pairs={{0,4},{4,0},{8,12},{12,8},{1,5},{5,1},{9,13},{13,9},{2,6},{6,2},{1... | collective-permute-start | bytes 61448 | tf_op jit(solution)/shard_map/ppermute | solution.py:117
  16.7 5.3 %collective-permute-start.5 = (f32[8,8,128]{2,1,0:T(8,128)S(1)}, f32[8,8,128]{2,1,0:T(8,128)S(1)}, u32[]{:S(2)}, u32[]{:S(2)}) collective-permute-start(f32[8,8,128]{2,1,0:T(8,128)S(1)} %get-tuple-element.59), channel_id=1, source_target_pairs={{0,1},{1,0},{2,3},{3,2},{4,5},{5,4},{6,7},{7,6},{8,9},{9,8},{10,11... | collective-permute-start | bytes 98312 | tf_op jit(solution)/shard_map/ppermute | solution.py:55
  18.3 3.9 %collective-permute-start.6 = (f32[8,8,128]{2,1,0:T(8,128)S(1)}, f32[8,8,128]{2,1,0:T(8,128)S(1)}, u32[]{:S(2)}, u32[]{:S(2)}) collective-permute-start(f32[8,8,128]{2,1,0:T(8,128)S(1)} %get-tuple-element.60), channel_id=1, source_target_pairs={{0,4},{1,2},{2,1},{3,7},{4,0},{5,6},{6,5},{7,3},{8,12},{9,10},{10,... | collective-permute-start | bytes 98312 | tf_op jit(solution)/shard_map/ppermute | solution.py:55
  19.7 3.8 %collective-permute-start.9 = (f32[5,8,128]{2,1,0:T(8,128)S(1)}, f32[5,8,128]{2,1,0:T(8,128)S(1)}, u32[]{:S(2)}, u32[]{:S(2)}) collective-permute-start(f32[5,8,128]{2,1,0:T(8,128)S(1)} %get-tuple-element.67.refs_0_), channel_id=1, source_target_pairs={{0,8},{4,12},{8,0},{12,4},{1,9},{5,13},{9,1},{13,5},{2,10},{6,14},... | collective-permute-start | bytes 61448 | tf_op jit(solution)/shard_map/ppermute | solution.py:117

commit v3 on v1

--- a/solution.py
+++ b/solution.py
@@ -152,8 +152,14 @@
 
 
 def spread(pack, lane, elems, slices, parts_ref, sums_ref):
-    for e in range(elems):
-        put_rows(parts_ref, e, jnp.stack([jnp.where(lane == e * slices + z, pack, 0.0) for z in range(slices)]))
+    cells, width = pack.shape
+    rows = slices * cells
+    halves = [part.astype(F32) for part in split(pack)]
+    for e in range(elems):
+        masks = [lane == e * slices + z for z in range(slices)]
+        for i, half in enumerate(halves):
+            flat = jnp.stack([jnp.where(mask, half, 0.0) for mask in masks]).reshape(rows, width)
+            parts_ref[e * rows : (e + 1) * rows, i * width : (i + 1) * width] = flat.astype(jnp.bfloat16)
     row_sums(parts_ref, sums_ref)
 
 

time: 24.8 us -> 24.7 us (level)
  no operation moved by 1% of the time
where the time goes in v3:
time: 24.7 us; the launch traced here: 24.5 us
  starting transfers between devices  13.7 us (55%)
  Pallas kernels  6.66 us (27%)
  waiting for transfers between devices  2.84 us (11%)
  between operations  1.37 us (6%)
    ppermute x4, starting transfers between devices, around(): other = lax.ppermute(block, axis, [(i, i ^ bit) for i in range(n)])  7.99 us
    pallas_call x11, Pallas kernels, call(): pl.pallas_call(body, out_shape=outs, in_specs=specs, out_specs=[pl.BlockS...  6.66 us
    ppermute x4, starting transfers between devices, swapped(): return lax.ppermute(block, ('path', 'gz'), route)  5.08 us
    ppermute x4, waiting for transfers between devices, around(): other = lax.ppermute(block, axis, [(i, i ^ bit) for i in range(n)])  1.65 us
    ppermute x4, waiting for transfers between devices, swapped(): return lax.ppermute(block, ('path', 'gz'), route)  0.94 us
    ppermute x2, starting transfers between devices, exchange_beam(): return [lax.ppermute(rows[0], 'beam', [(0, 1), (1, 0)])]  0.59 us
  transfers between devices with their start and end apart: 10, of which 5 were waited for; matrix products, arithmetic and copies ran while one was open for 0% of the time, Pallas kernels for 10%

profile of v3, /device:TPU:0, one launch (start us, length us, event | category | flops | bytes accessed | tf_op | source)
XLA Modules:
  0.0 24.5 jit_solution(14418184116343041386)
XLA Ops:
  1.3 1.2 %shard_map.94 = (f32[8,16,8,128]{3,2,1,0:T(8,128)S(1)}, f32[16,8,128]{2,1,0:T(8,128)S(1)}, f32[72,128]{1,0:T(8,128)S(1)}, f32[144,128]{1,0:T(8,128)S(1)}) custom-call(s32[1,1]{1,0:T(1,128)} %bitcast.5.view_ref, f32[8,16,8,128]{3,2,1,0:T(8,128)} %source_ref.1, f32[8,8]{1,0:T(8,128)} %refs_0_.1, f32[8,16]{1,0:T(8,128)} %bitcast.7, s32[8]{0:T(128)} %refs_2_.1, ...), custom_call_target="tpu_custom_call" | custom-call | flops 1000000 | bytes 1225540 | tf_op jit(solution)/shard_map/pallas_call | solution.py:26
  2.5 0.5 %collective-permute-start = (f32[144,128]{1,0:T(8,128)S(1)}, f32[144,128]{1,0:T(8,128)S(1)}, u32[]{:S(2)}, u32[]{:S(2)}) collective-permute-start(f32[144,128]{1,0:T(8,128)S(1)} %get-tuple-element.39.refs_0_), channel_id=1, source_target_pairs={{0,16},{16,0},{1,17},{17,1},{2,18},{18,2},{3,19},{19,3},{4,20},{20... | collective-permute-start | bytes 221192 | tf_op jit(solution)/shard_map/ppermute | solution.py:221
  3.0 0.7 %shard_map.95 = (f32[8,16,8,128]{3,2,1,0:T(8,128)S(1)}, f32[4,8,128]{2,1,0:T(8,128)S(1)}) custom-call(f32[8,16,8,128]{3,2,1,0:T(8,128)S(1)} %get-tuple-element.37.maps_ref, f32[72,128]{1,0:T(8,128)S(1)} %get-tuple-element.40.coef_ref), custom_call_target="tpu_custom_call" | custom-call | flops 1000000 | bytes 1101824 | tf_op jit(solution)/shard_map/pallas_call | solution.py:26
  3.6 0.3 %collective-permute-done.carry_ref.refs_1_ = f32[144,128]{1,0:T(8,128)S(1)} collective-permute-done((f32[144,128]{1,0:T(8,128)S(1)}, f32[144,128]{1,0:T(8,128)S(1)}, u32[]{:S(2)}, u32[]{:S(2)}) %collective-permute-start) | collective-permute-done | bytes 73760 | tf_op jit(solution)/shard_map/ppermute | solution.py:221
  3.9 0.5 %shard_map.96 = (f32[8,16,8,128]{3,2,1,0:T(8,128)S(1)}, f32[5,8,128]{2,1,0:T(8,128)S(1)}, f32[8,8,128]{2,1,0:T(8,128)S(1)}, f32[8,8,128]{2,1,0:T(8,128)S(1)}) custom-call(f32[8,16,8,128]{3,2,1,0:T(8,128)S(1)} %get-tuple-element.37.maps_ref, f32[16,8,128]{2,1,0:T(8,128)S(1)} %get-tuple-element.38.inside_ref, ...), custom_call_target="tpu_custom_call" | custom-call | flops 1000000 | bytes 1814528 | tf_op jit(solution)/shard_map/pallas_call | solution.py:26
  4.4 0.0 copy-start
  4.4 2.9 %collective-permute-start.3 = (f32[5,8,128]{2,1,0:T(8,128)S(1)}, f32[5,8,128]{2,1,0:T(8,128)S(1)}, u32[]{:S(2)}, u32[]{:S(2)}) collective-permute-start(f32[5,8,128]{2,1,0:T(8,128)S(1)} %get-tuple-element.46.refs_1_.pack_ref), channel_id=1, source_target_pairs={{0,4},{4,0},{8,12},{12,8},{1,5},{5,1},{9,13},{13,9},{2,6},{6,2},{1... | collective-permute-start | bytes 61448 | tf_op jit(solution)/shard_map/ppermute | solution.py:116
  7.3 1.6 %collective-permute-start.1 = (f32[8,8,128]{2,1,0:T(8,128)S(1)}, f32[8,8,128]{2,1,0:T(8,128)S(1)}, u32[]{:S(2)}, u32[]{:S(2)}) collective-permute-start(f32[8,8,128]{2,1,0:T(8,128)S(1)} %get-tuple-element.47), channel_id=1, source_target_pairs={{0,1},{1,0},{2,3},{3,2},{4,5},{5,4},{6,7},{7,6},{8,9},{9,8},{10,11... | collective-permute-start | bytes 98312 | tf_op jit(solution)/shard_map/ppermute | solution.py:54
  8.9 0.5 %collective-permute-start.2 = (f32[8,8,128]{2,1,0:T(8,128)S(1)}, f32[8,8,128]{2,1,0:T(8,128)S(1)}, u32[]{:S(2)}, u32[]{:S(2)}) collective-permute-start(f32[8,8,128]{2,1,0:T(8,128)S(1)} %get-tuple-element.48), channel_id=1, source_target_pairs={{0,4},{1,2},{2,1},{3,7},{4,0},{5,6},{6,5},{7,3},{8,12},{9,10},{10,... | collective-permute-start | bytes 98312 | tf_op jit(solution)/shard_map/ppermute | solution.py:54
  9.4 0.0 collective-permute-done.3.refs_2_
  9.4 1.8 %collective-permute-start.4 = (f32[5,8,128]{2,1,0:T(8,128)S(1)}, f32[5,8,128]{2,1,0:T(8,128)S(1)}, u32[]{:S(2)}, u32[]{:S(2)}) collective-permute-start(f32[5,8,128]{2,1,0:T(8,128)S(1)} %get-tuple-element.49.refs_0_), channel_id=1, source_target_pairs={{0,8},{4,12},{8,0},{12,4},{1,9},{5,13},{9,1},{13,5},{2,10},{6,14},... | collective-permute-start | bytes 61448 | tf_op jit(solution)/shard_map/ppermute | solution.py:116
  11.2 0.0 copy-done
  11.2 0.8 %shard_map.97 = (f32[8,16,8,128]{3,2,1,0:T(8,128)S(1)}, f32[8,16,8,128]{3,2,1,0:T(8,128)S(1)}, f32[8,16,8,128]{3,2,1,0:T(8,128)S(1)}, f32[8,16,8,128]{3,2,1,0:T(...) custom-call(f32[8,16,8,128]{3,2,1,0:T(8,128)S(1)} %get-tuple-element.37.maps_ref, f32[8,8,16]{2,1,0:T(8,128)S(1)} %bitcast.6, ...), custom_call_target="tpu_custom_call" | custom-call | flops 1000000 | bytes 2842624 | tf_op jit(solution)/shard_map/pallas_call | solution.py:26
  12.0 0.0 collective-permute-done.1.zone_ref
  12.0 0.8 %collective-permute-done.2.ztwo_ref = f32[8,8,128]{2,1,0:T(8,128)S(1)} collective-permute-done((f32[8,8,128]{2,1,0:T(8,128)S(1)}, f32[8,8,128]{2,1,0:T(8,128)S(1)}, u32[]{:S(2)}, u32[]{:S(2)}) %collective-permute-start.2) | collective-permute-done | bytes 32800 | tf_op jit(solution)/shard_map/ppermute | solution.py:54
  12.8 0.5 %collective-permute-done.4.refs_1_ = f32[5,8,128]{2,1,0:T(8,128)S(1)} collective-permute-done((f32[5,8,128]{2,1,0:T(8,128)S(1)}, f32[5,8,128]{2,1,0:T(8,128)S(1)}, u32[]{:S(2)}, u32[]{:S(2)}) %collective-permute-start.4) | collective-permute-done | bytes 20512 | tf_op jit(solution)/shard_map/ppermute | solution.py:116
  13.3 1.4 %shard_map.99 = (f32[8,16,8,128]{3,2,1,0:T(8,128)S(1)}, f32[8,16,8,128]{3,2,1,0:T(8,128)S(1)}, f32[8,16,8,128]{3,2,1,0:T(8,128)S(1)}, f32[8,16,8,128]{3,2,1,0:T(...) custom-call(f32[8,16,8,128]{3,2,1,0:T(8,128)S(1)} %get-tuple-element, ...), custom_call_target="tpu_custom_call" | custom-call | flops 1000000 | bytes 3936256 | tf_op jit(solution)/shard_map/pallas_call | solution.py:26
  14.7 0.1 shard_map.101
  14.7 0.1 collective-permute-start.7
  14.8 1.7 %collective-permute-start.8 = (f32[5,8,128]{2,1,0:T(8,128)S(1)}, f32[5,8,128]{2,1,0:T(8,128)S(1)}, u32[]{:S(2)}, u32[]{:S(2)}) collective-permute-start(f32[5,8,128]{2,1,0:T(8,128)S(1)} %get-tuple-element.66.refs_0_.own_pack_ref), channel_id=1, source_target_pairs={{0,4},{4,0},{8,12},{12,8},{1,5},{5,1},{9,13},{13,9},{2,6},{6,2},{1... | collective-permute-start | bytes 61448 | tf_op jit(solution)/shard_map/ppermute | solution.py:116
  16.6 1.6 %collective-permute-start.5 = (f32[8,8,128]{2,1,0:T(8,128)S(1)}, f32[8,8,128]{2,1,0:T(8,128)S(1)}, u32[]{:S(2)}, u32[]{:S(2)}) collective-permute-start(f32[8,8,128]{2,1,0:T(8,128)S(1)} %get-tuple-element.59), channel_id=1, source_target_pairs={{0,1},{1,0},{2,3},{3,2},{4,5},{5,4},{6,7},{7,6},{8,9},{9,8},{10,11... | collective-permute-start | bytes 98312 | tf_op jit(solution)/shard_map/ppermute | solution.py:54
  18.1 1.4 %collective-permute-start.6 = (f32[8,8,128]{2,1,0:T(8,128)S(1)}, f32[8,8,128]{2,1,0:T(8,128)S(1)}, u32[]{:S(2)}, u32[]{:S(2)}) collective-permute-start(f32[8,8,128]{2,1,0:T(8,128)S(1)} %get-tuple-element.60), channel_id=1, source_target_pairs={{0,4},{1,2},{2,1},{3,7},{4,0},{5,6},{6,5},{7,3},{8,12},{9,10},{10,... | collective-permute-start | bytes 98312 | tf_op jit(solution)/shard_map/ppermute | solution.py:54
  19.5 0.0 collective-permute-done.8.refs_1_
  19.5 1.6 %collective-permute-start.9 = (f32[5,8,128]{2,1,0:T(8,128)S(1)}, f32[5,8,128]{2,1,0:T(8,128)S(1)}, u32[]{:S(2)}, u32[]{:S(2)}) collective-permute-start(f32[5,8,128]{2,1,0:T(8,128)S(1)} %get-tuple-element.67.refs_0_), channel_id=1, source_target_pairs={{0,8},{4,12},{8,0},{12,4},{1,9},{5,13},{9,1},{13,5},{2,10},{6,14},... | collective-permute-start | bytes 61448 | tf_op jit(solution)/shard_map/ppermute | solution.py:116
  21.1 0.7 %shard_map.100.adj_ref = f32[8,16,8,128]{3,2,1,0:T(8,128)S(1)} custom-call(f32[8,16,8,128]{3,2,1,0:T(8,128)S(1)} %get-tuple-element.53.ext_ref, f32[8,16,8,128]{3,2,1,0:T(8,128)S(1)} %get-tuple-element.55.dual_z_ref, f32[8,16,8,128]{3,2,1,0:T(8,128)S(1)} %get-tuple-element.56.dual_x_ref, f32[8,16,8,128]{3,2,1,0:T(8,128)S(1)} %get-tuple-element.57.dual_y_ref), custom_call_target="tpu_custom_call" | custom-call | flops 1000000 | bytes 2621440 | tf_op jit(solution)/shard_map/pallas_call | solution.py:26
  21.9 0.0 collective-permute-done.5.zone_ref
  21.9 0.2 collective-permute-done.6.ztwo_ref
  22.1 0.0 collective-permute-done.7.refs_2_
  22.1 0.2 shard_map.102.base_ref
  22.2 1.2 %collective-permute-done.9.refs_1_ = f32[5,8,128]{2,1,0:T(8,128)S(1)} collective-permute-done((f32[5,8,128]{2,1,0:T(8,128)S(1)}, f32[5,8,128]{2,1,0:T(8,128)S(1)}, u32[]{:S(2)}, u32[]{:S(2)}) %collective-permute-start.9) | collective-permute-done | bytes 20512 | tf_op jit(solution)/shard_map/ppermute | solution.py:116
  23.4 1.1 %shard_map.104 = (f32[8,16,8,128]{3,2,1,0:T(8,128)}, f32[8,8,16]{2,1,0:T(8,128)}) custom-call(f32[8,16,8,128]{3,2,1,0:T(8,128)S(1)} %shard_map.102.base_ref, f32[8,16,8,128]{3,2,1,0:T(8,128)S(1)} %get-tuple-element.63.pull_ref, f32[8,16,8,128]{3,2,1,0:T(8,128)S(1)} %get-tuple-element.54.tau_ref, f32[8,128]{1,0:T(8,128)S(1)} %get-tuple-element.45.still_ref, ...), custom_call_target="tpu_custom_call" | custom-call | flops 1000000 | bytes 2191360 | tf_op jit(solution)/shard_map/pallas_call | solution.py:26
  (2 shorter events, 0.0 us)
Async XLA Ops:
  2.5 1.4 %collective-permute-start = (f32[144,128]{1,0:T(8,128)S(1)}, f32[144,128]{1,0:T(8,128)S(1)}, u32[]{:S(2)}, u32[]{:S(2)}) collective-permute-start(f32[144,128]{1,0:T(8,128)S(1)} %get-tuple-element.39.refs_0_), channel_id=1, source_target_pairs={{0,16},{16,0},{1,17},{17,1},{2,18},{18,2},{3,19},{19,3},{4,20},{20... | collective-permute-start | bytes 221192 | tf_op jit(solution)/shard_map/ppermute | solution.py:221
  4.4 6.8 %copy-start = (f32[8,16,8]{1,2,0:T(8,128)S(1)}, f32[8,16,8]{1,2,0:T(8,128)}, u32[]{:S(2)}) copy-start(f32[8,16,8]{1,2,0:T(8,128)} %param.8) | copy-start | bytes 12292
  4.4 5.0 %collective-permute-start.3 = (f32[5,8,128]{2,1,0:T(8,128)S(1)}, f32[5,8,128]{2,1,0:T(8,128)S(1)}, u32[]{:S(2)}, u32[]{:S(2)}) collective-permute-start(f32[5,8,128]{2,1,0:T(8,128)S(1)} %get-tuple-element.46.refs_1_.pack_ref), channel_id=1, source_target_pairs={{0,4},{4,0},{8,12},{12,8},{1,5},{5,1},{9,13},{13,9},{2,6},{6,2},{1... | collective-permute-start | bytes 61448 | tf_op jit(solution)/shard_map/ppermute | solution.py:116
  7.3 4.7 %collective-permute-start.1 = (f32[8,8,128]{2,1,0:T(8,128)S(1)}, f32[8,8,128]{2,1,0:T(8,128)S(1)}, u32[]{:S(2)}, u32[]{:S(2)}) collective-permute-start(f32[8,8,128]{2,1,0:T(8,128)S(1)} %get-tuple-element.47), channel_id=1, source_target_pairs={{0,1},{1,0},{2,3},{3,2},{4,5},{5,4},{6,7},{7,6},{8,9},{9,8},{10,11... | collective-permute-start | bytes 98312 | tf_op jit(solution)/shard_map/ppermute | solution.py:54
  8.9 3.9 %collective-permute-start.2 = (f32[8,8,128]{2,1,0:T(8,128)S(1)}, f32[8,8,128]{2,1,0:T(8,128)S(1)}, u32[]{:S(2)}, u32[]{:S(2)}) collective-permute-start(f32[8,8,128]{2,1,0:T(8,128)S(1)} %get-tuple-element.48), channel_id=1, source_target_pairs={{0,4},{1,2},{2,1},{3,7},{4,0},{5,6},{6,5},{7,3},{8,12},{9,10},{10,... | collective-permute-start | bytes 98312 | tf_op jit(solution)/shard_map/ppermute | solution.py:54
  9.4 3.8 %collective-permute-start.4 = (f32[5,8,128]{2,1,0:T(8,128)S(1)}, f32[5,8,128]{2,1,0:T(8,128)S(1)}, u32[]{:S(2)}, u32[]{:S(2)}) collective-permute-start(f32[5,8,128]{2,1,0:T(8,128)S(1)} %get-tuple-element.49.refs_0_), channel_id=1, source_target_pairs={{0,8},{4,12},{8,0},{12,4},{1,9},{5,13},{9,1},{13,5},{2,10},{6,14},... | collective-permute-start | bytes 61448 | tf_op jit(solution)/shard_map/ppermute | solution.py:116
  14.7 7.3 %collective-permute-start.7 = (f32[128,128]{1,0:T(8,128)S(1)}, f32[128,128]{1,0:T(8,128)S(1)}, u32[]{:S(2)}, u32[]{:S(2)}) collective-permute-start(f32[128,128]{1,0:T(8,128)S(1)} %get-tuple-element.62.refs_1_), channel_id=1, source_target_pairs={{0,16},{16,0},{1,17},{17,1},{2,18},{18,2},{3,19},{19,3},{4,20},{20... | collective-permute-start | bytes 196616 | tf_op jit(solution)/shard_map/ppermute | solution.py:221
  14.8 4.7 %collective-permute-start.8 = (f32[5,8,128]{2,1,0:T(8,128)S(1)}, f32[5,8,128]{2,1,0:T(8,128)S(1)}, u32[]{:S(2)}, u32[]{:S(2)}) collective-permute-start(f32[5,8,128]{2,1,0:T(8,128)S(1)} %get-tuple-element.66.refs_0_.own_pack_ref), channel_id=1, source_target_pairs={{0,4},{4,0},{8,12},{12,8},{1,5},{5,1},{9,13},{13,9},{2,6},{6,2},{1... | collective-permute-start | bytes 61448 | tf_op jit(solution)/shard_map/ppermute | solution.py:116
  16.6 5.3 %collective-permute-start.5 = (f32[8,8,128]{2,1,0:T(8,128)S(1)}, f32[8,8,128]{2,1,0:T(8,128)S(1)}, u32[]{:S(2)}, u32[]{:S(2)}) collective-permute-start(f32[8,8,128]{2,1,0:T(8,128)S(1)} %get-tuple-element.59), channel_id=1, source_target_pairs={{0,1},{1,0},{2,3},{3,2},{4,5},{5,4},{6,7},{7,6},{8,9},{9,8},{10,11... | collective-permute-start | bytes 98312 | tf_op jit(solution)/shard_map/ppermute | solution.py:54
  18.1 3.9 %collective-permute-start.6 = (f32[8,8,128]{2,1,0:T(8,128)S(1)}, f32[8,8,128]{2,1,0:T(8,128)S(1)}, u32[]{:S(2)}, u32[]{:S(2)}) collective-permute-start(f32[8,8,128]{2,1,0:T(8,128)S(1)} %get-tuple-element.60), channel_id=1, source_target_pairs={{0,4},{1,2},{2,1},{3,7},{4,0},{5,6},{6,5},{7,3},{8,12},{9,10},{10,... | collective-permute-start | bytes 98312 | tf_op jit(solution)/shard_map/ppermute | solution.py:54
  19.5 3.8 %collective-permute-start.9 = (f32[5,8,128]{2,1,0:T(8,128)S(1)}, f32[5,8,128]{2,1,0:T(8,128)S(1)}, u32[]{:S(2)}, u32[]{:S(2)}) collective-permute-start(f32[5,8,128]{2,1,0:T(8,128)S(1)} %get-tuple-element.67.refs_0_), channel_id=1, source_target_pairs={{0,8},{4,12},{8,0},{12,4},{1,9},{5,13},{9,1},{13,5},{2,10},{6,14},... | collective-permute-start | bytes 61448 | tf_op jit(solution)/shard_map/ppermute | solution.py:116
